TPU v7x, 32 devices: a whole 2x2x4 slice. The times are simulated.
32 devices in a mesh: grp: 4 (over y, core), req: 8 (over z, x).
Axes of the slice: x: 2, y: 2, z: 4, core: 2. Of those that a mesh axis runs over, the one named last changes fastest.
Arguments:
- tokens: bfloat16 [4096, 1024], P(('grp', 'req')), may hold values from -6 to 6
- attn_gain: float32 [1024], replicated, may hold values from 0.1 to 1.9
- w_query: bfloat16 [1024, 1024], replicated, may hold values from -0.0234375 to 0.0234375
- w_key: bfloat16 [1024, 1024], replicated, may hold values from -0.1875 to 0.1875
- w_value: bfloat16 [1024, 1024], replicated, may hold values from -0.1875 to 0.1875
- w_attn_out: bfloat16 [1024, 1024], replicated, may hold values from -0.1875 to 0.1875
- rel_bias: float32 [32, 16], replicated, may hold values from -4 to 4
- prefix_cache: bfloat16 [8, 512, 2048], P('grp', 'req'), may hold values from -6 to 6
- lengths: int32 [4, 16], P('grp'), may hold values from 1 to 128, 1024 in all within a row
- prefix_map: int32 [4, 16], P('grp'), may hold values from 0 to 1
- mlp_gain: float32 [1024], replicated, may hold values from 0.1 to 1.9
- w_in: bfloat16 [4096, 1024], P('grp'), may hold values from -0.1875 to 0.1875
- w_out: bfloat16 [4096, 1024], P('grp'), may hold values from -0.09375 to 0.09375
Outputs:
- layer_out: bfloat16 [4096, 1024], P(('grp', 'req'))
Inputs may be any that keep to these rules, and one draw needn't show every extreme that they name: In each group the lengths sum to 1024 and the longest is exactly 128.
All inputs are finite; a program needn't handle non-finite values.
Results may differ from a plain program's by a relative error of at most 0.017.
Values may be sent and summed in bfloat16 or wider, within the bound.
A program may use at most 128 MiB of HBM per device.

v0:
```python
import jax
import jax.numpy as jnp
from jax import lax
from jax.sharding import PartitionSpec as P

D = 1024
H = 16
DK = 64
PLEN = 512
PREF_GRP = 2


epsilon = 1e-06
far_marks = (12, 16, 23, 32, 46, 64, 91)
masked_score = -1e30


def padded(value, sides, width):
    for axis, dim in sides:
        count, length = (lax.axis_size(axis), value.shape[dim])
        up = [(i, (i + 1) % count) for i in range(count - 1)]
        down = [(j, i) for i, j in up]
        last = lax.slice_in_dim(value, length - width, length, axis=dim)
        leading = lax.slice_in_dim(value, 0, width, axis=dim)
        before = lax.ppermute(last, axis, up)
        after = lax.ppermute(leading, axis, down)
        value = jnp.concatenate([before, value, after], axis=dim)
    return value


def bucket_of(relative):
    distance = jnp.abs(relative)
    far_bucket = 8 + sum([(distance >= threshold).astype(jnp.int32) for threshold in far_marks])
    bucket = jnp.where(distance < 8, distance, far_bucket)
    return bucket + jnp.where(relative > 0, 16, 0)


def bias_lookup(relative, rel_bias):
    buckets = bucket_of(relative)
    marks = jnp.arange(rel_bias.shape[0], dtype=jnp.int32)
    one_hot = (buckets[:, :, None] == marks[None, None, :]).astype(jnp.float32)
    return jnp.einsum(
        "qkb,bh->hqk",
        one_hot,
        rel_bias,
        precision=lax.Precision.HIGHEST,
        preferred_element_type=jnp.float32,
    )


def norm_rows(values_in, gain):
    widened = values_in.astype(jnp.float32)
    scale = lax.rsqrt(jnp.mean(widened * widened, axis=-1, keepdims=True) + epsilon)
    return (widened * scale * gain).astype(jnp.bfloat16)


def layout(lengths_row, prefix_row, row_ids):
    req_ends = jnp.cumsum(lengths_row)
    req_starts = req_ends - lengths_row
    member = (
        (row_ids[:, None] >= req_starts[None, :]) & (row_ids[:, None] < req_ends[None, :])
    ).astype(jnp.int32)
    numbers = jnp.arange(lengths_row.shape[0], dtype=jnp.int32)
    req_index = jnp.sum(member * numbers[None, :], axis=1) + jnp.sum(member, axis=1) - 1
    offset = row_ids - jnp.sum(member * req_starts[None, :], axis=1)
    chosen = jnp.sum(member * prefix_row[None, :], axis=1)
    return (req_index, offset, chosen)


def softmax_part(scores, value_rows, allowed):
    scores = jnp.where(allowed[None], scores, masked_score)
    row_max = jnp.max(scores, axis=2)
    exp_terms = jnp.where(allowed[None], jnp.exp(scores - row_max[:, :, None]), 0.0)
    row_sum = jnp.sum(exp_terms, axis=2)
    weighted = jnp.einsum(
        "hqk,khd->hqd",
        exp_terms.astype(jnp.bfloat16),
        value_rows,
        preferred_element_type=jnp.float32,
    )
    return (row_max, row_sum, weighted)


def combine(first_part, second_part):
    row_max = jnp.maximum(first_part[0], second_part[0])
    scale_one = jnp.exp(first_part[0] - row_max)
    scale_two = jnp.exp(second_part[0] - row_max)
    row_sum = first_part[1] * scale_one + second_part[1] * scale_two
    weighted = first_part[2] * scale_one[:, :, None] + second_part[2] * scale_two[:, :, None]
    return (row_max, row_sum, weighted)


def feed_forward(rows_in, in_part, out_part):
    units = lax.dot_general(
        rows_in, in_part, (((1,), (1,)), ((), ())), preferred_element_type=jnp.float32
    )
    units = jnp.maximum(units, 0.0).astype(jnp.bfloat16)
    return jnp.dot(units, out_part, preferred_element_type=jnp.float32)


def body(
    tokens,
    attn_gain,
    w_query,
    w_key,
    w_value,
    w_attn_out,
    rel_bias,
    prefix_cache,
    lengths,
    prefix_map,
    mlp_gain,
    w_in,
    w_out,
):
    rows_here = tokens.shape[0]
    device_pos = lax.axis_index("req")
    group_lengths = lengths[0]
    group_map = prefix_map[0]
    normed = norm_rows(tokens, attn_gain)
    query = (
        jnp.dot(normed, w_query, preferred_element_type=jnp.float32)
        .astype(jnp.bfloat16)
        .reshape(rows_here, H, DK)
    )
    key_value = jnp.concatenate(
        [
            jnp.dot(normed, w_key, preferred_element_type=jnp.float32).astype(jnp.bfloat16),
            jnp.dot(normed, w_value, preferred_element_type=jnp.float32).astype(jnp.bfloat16),
        ],
        axis=1,
    )
    query_ids = device_pos * rows_here + jnp.arange(rows_here, dtype=jnp.int32)
    query_req, query_offset, query_prefix = layout(group_lengths, group_map, query_ids)
    all_positions = jnp.arange(PLEN, dtype=jnp.int32)
    prefix_bias = bias_lookup(all_positions[None, :] - PLEN - query_offset[:, None], rel_bias)
    empty_state = (
        jnp.full((H, rows_here), masked_score, jnp.float32),
        jnp.zeros((H, rows_here), jnp.float32),
        jnp.zeros((H, rows_here, DK), jnp.float32),
    )
    running = empty_state
    shard_kv = lax.all_gather(prefix_cache, "req", axis=1, tiled=True)
    prefix_ids = jnp.arange(PREF_GRP, dtype=jnp.int32)
    slices = shard_kv.shape[0]
    piece_len = shard_kv.shape[1]
    step_len = max(min(piece_len, 512 // slices), 1)
    for begin in range(0, piece_len, step_len):
        width = min(step_len, piece_len - begin)
        block = shard_kv[:, begin : begin + width]
        key_rows = block[:, :, :D].reshape(slices, width, H, DK)
        value_rows = block[:, :, D:].reshape(-1, H, DK)
        rel_terms = lax.dynamic_slice_in_dim(prefix_bias, begin, width, 2)
        prefix_scores = jnp.einsum(
            "qhd,swhd->hqsw", query, key_rows, preferred_element_type=jnp.float32
        )
        prefix_scores = (prefix_scores + rel_terms[:, :, None, :]).reshape(
            H, rows_here, slices * width
        )
        allowed = jnp.repeat(query_prefix[:, None] == prefix_ids[None, :], width, axis=1)
        running = combine(running, softmax_part(prefix_scores, value_rows, allowed))
    state = running
    window = padded(key_value, (("req", 0),), rows_here)
    window_ids = device_pos * rows_here - rows_here + jnp.arange(3 * rows_here, dtype=jnp.int32)
    window_req = layout(group_lengths, group_map, window_ids)[0]
    for part_idx in range(3):
        part_rows = window[part_idx * rows_here : (part_idx + 1) * rows_here]
        part_ids = window_ids[part_idx * rows_here : (part_idx + 1) * rows_here]
        part_req = window_req[part_idx * rows_here : (part_idx + 1) * rows_here]
        suffix_terms = bias_lookup(part_ids[None, :] - query_ids[:, None], rel_bias)
        suffix_allowed = part_req[None, :] == query_req[:, None]
        scores = (
            jnp.einsum(
                "qhd,khd->hqk",
                query,
                part_rows[:, :D].reshape(-1, H, DK),
                preferred_element_type=jnp.float32,
            )
            + suffix_terms
        )
        suffix_state = softmax_part(scores, part_rows[:, D:].reshape(-1, H, DK), suffix_allowed)
        state = combine(state, suffix_state)
    attended = (
        (state[2] / state[1][:, :, None])
        .transpose(1, 0, 2)
        .reshape(rows_here, D)
        .astype(jnp.bfloat16)
    )
    hidden_one = (
        tokens.astype(jnp.float32)
        + jnp.dot(attended, w_attn_out, preferred_element_type=jnp.float32)
    ).astype(jnp.bfloat16)
    normed_two = norm_rows(hidden_one, mlp_gain)
    gathered = lax.all_gather(normed_two, "grp", axis=0, tiled=True)
    mlp_total = lax.psum_scatter(
        feed_forward(gathered, w_in, w_out).astype(jnp.bfloat16),
        "grp",
        scatter_dimension=0,
        tiled=True,
    ).astype(jnp.float32)
    return (hidden_one.astype(jnp.float32) + mlp_total).astype(jnp.bfloat16)


def solution(mesh):
    return jax.shard_map(
        body,
        mesh=mesh,
        in_specs=(
            P(("grp", "req"), None),
            P(),
            P(),
            P(),
            P(),
            P(),
            P(),
            P("grp", "req", None),
            P("grp", None),
            P("grp", None),
            P(),
            P("grp", None),
            P("grp", None),
        ),
        out_specs=P(("grp", "req"), None),
        check_vma=False,
    )
```

profile of v0, /device:TPU:0, one launch (start us, length us, event | category | flops | bytes accessed | tf_op | source)
XLA Modules:
  0.0 213.8 jit_solution(10497205921933201642)
XLA Ops:
  6.5 2.5 %copy.91 = bf16[2,64,2048]{2,0,1:T(2,128)(2,1)} copy(bf16[2,64,2048]{2,1,0:T(8,128)(2,1)} %param.20) | data formatting | bytes 1048576 | tf_op args[7]
  9.2 1.2 fusion.46
  10.4 2.2 %convolution_convert_fusion.1 = bf16[128,1024]{1,0:T(8,128)(2,1)S(1)} fusion(bf16[1024,1024]{1,0:T(8,128)(2,1)} %param.17, bf16[128,1024]{1,0:T(8,128)(2,1)} %param.13, f32[1024]{0:T(1024)} %param.14, f32[128]{0:T(128)S(1)} %add_rsqrt_fusion.1), kind=kOutput, calls=%fused_computation.56 | convolution fusion | flops 269090816 | bytes 2626048 | tf_op jit(solution)/shard_map/dot_general | solution.py:129
  12.7 0.5 convolution_convert_fusion.2
  13.4 0.8 pad_maximum_fusion
  14.2 1.4 collective-permute-start.1
  15.6 6.3 %collective-permute-start = (bf16[128,2048]{1,0:T(8,128)(2,1)}, bf16[128,2048]{1,0:T(8,128)(2,1)}, u32[]{:S(2)}, u32[]{:S(2)}) collective-permute-start(bf16[128,2048]{1,0:T(8,128)(2,1)} %pad_maximum_fusion), channel_id=1, source_target_pairs={{0,1},{1,2},{2,3},{3,4},{4,5},{5,6},{6,7},{8,9},{9,10},{10,11},{11... | collective-permute-start | bytes 1572872 | tf_op jit(solution)/shard_map/ppermute | solution.py:25
  21.9 0.8 copy.108
  22.7 2.1 convolution_convert_fusion.3
  25.3 0.9 fusion.90
  26.2 0.7 fusion.12
  26.9 1.4 copy.109
  28.7 0.3 fusion.68
  29.1 2.6 %fusion.13 = f32[128,128,16]{1,2,0:T(8,128)} fusion(s32[128,128]{1,0:T(8,128)} %get-tuple-element.57, f32[32,16]{0,1:T(8,128)S(1)} %copy-done.20), kind=kOutput, calls=%fused_computation.26 | convolution fusion | flops 101187584 | bytes 1116160 | tf_op jit(solution)/shard_map/qkb,bh->hqk/dot_general | solution.py:42
  31.6 1.3 fusion.137
  32.9 3.0 %fusion.10 = f32[16,128,512]{2,0,1:T(8,128)S(1)} fusion(s32[128,512]{1,0:T(8,128)S(1)} %fusion.68, f32[32,16]{0,1:T(8,128)S(1)} %copy-done.20), kind=kOutput, calls=%fused_computation.17 | convolution fusion | flops 404750336 | bytes 4458496 | tf_op jit(solution)/shard_map/qkb,bh->hqk/dot_general | solution.py:42
  35.9 2.7 %fusion.131 = (f32[16,128,256]{2,0,1:T(8,128)}, f32[16,128,256]{2,0,1:T(8,128)}) fusion(f32[16,128,512]{2,0,1:T(8,128)S(1)} %fusion.10), kind=kLoop, calls=%fused_computation.204 | loop fusion | bytes 8388608 | tf_op jit(solution)/shard_map/dynamic_slice | solution.py:153
  38.6 1.8 fusion.11
  40.6 1.8 copy.110
  42.4 2.6 %copy.113 = f32[128,128,16]{0,1,2:T(8,128)} copy(f32[128,128,16]{1,2,0:T(8,128)} %fusion.13) | data formatting | bytes 2097152 | tf_op jit(solution)/shard_map/qkb,bh->hqk/dot_general | solution.py:42
  45.0 4.1 %copy.94 = f32[16,128,256]{2,1,0:T(8,128)} copy(f32[16,128,256]{2,0,1:T(8,128)} %get-tuple-element.28) | data formatting | bytes 4194304 | tf_op jit(solution)/shard_map/dynamic_slice | solution.py:153
  49.1 2.5 %copy.105 = f32[128,128,16]{0,1,2:T(8,128)} copy(f32[128,128,16]{1,2,0:T(8,128)} %fusion.11) | data formatting | bytes 2097152 | tf_op jit(solution)/shard_map/qkb,bh->hqk/dot_general | solution.py:42
  51.7 4.2 %copy.100 = f32[16,128,256]{2,1,0:T(8,128)} copy(f32[16,128,256]{2,0,1:T(8,128)} %get-tuple-element.29) | data formatting | bytes 4194304 | tf_op jit(solution)/shard_map/dynamic_slice | solution.py:153
  55.8 1.8 fusion.133
  57.7 1.8 copy.114
  59.5 1.8 copy.112
  61.3 1.8 fusion.132
  63.2 1.8 copy.104
  65.0 1.8 copy.106
  66.8 2.0 fusion.136
  68.7 1.0 copy-done.3
  69.9 0.4 fusion.138
  70.3 1.0 copy-done.7
  71.4 0.2 fusion.40
  71.6 28.4 %all-gather.3.cloned.1.call-done = bf16[2,512,2048]{2,0,1:T(2,128)(2,1)} async-done(((bf16[2,64,2048]{2,0,1:T(2,128)(2,1)}), bf16[2,512,2048]{2,0,1:T(2,128)(2,1)}) %all-gather.3.cloned.1.call-update) | async-done | bytes 4194320 | tf_op jit(solution)/shard_map/all_gather | solution.py:143
  100.0 5.7 %fusion.130 = (bf16[2,256,1024]{2,0,1:T(2,128)(2,1)}, bf16[2,256,1024]{2,0,1:T(2,128)(2,1)}, bf16[2,256,1024]{2,0,1:T(2,128)(2,1)}, bf16[2,256,1024]{2,0,1:T(2,128)(2,1)}) fusion(bf16[2,512,2048]{2,0,1:T(2,128)(2,1)} %all-gather.3.cloned.1.call-done), kind=kLoop, calls=%fused_computation.203 | loop fusion | bytes 8388608 | tf_op jit(solution)/shard_map/slice | solution.py:152
  105.7 3.6 %copy.122 = bf16[2,256,1024]{1,2,0:T(8,128)(2,1)} copy(bf16[2,256,1024]{2,0,1:T(2,128)(2,1)} %get-tuple-element.25) | data formatting | bytes 2097152
  109.3 3.7 %copy.123 = bf16[2,256,1024]{1,2,0:T(8,128)(2,1)} copy(bf16[2,256,1024]{2,0,1:T(2,128)(2,1)} %get-tuple-element.27) | data formatting | bytes 2097152
  113.0 2.9 %select_reduce_fusion.3 = (f32[16,128]{1,0:T(8,128)S(1)}, f32[16,128,2,256]{3,1,2,0:T(8,128)S(1)}) fusion(pred[128,2]{0,1:T(4,128)(4,1)S(1)} %iota_compare_fusion.10, f32[16,128,256]{2,1,0:T(8,128)} %copy.94, bf16[128,16,64,1]{0,2,3,1:T(8,128)(2,1)S(1)} %bitcast.213, bf16[2,256,16,64]{1,3,2,0:T(8,128)(2,1)} %bitcast.215), kind=kOutput, calls=%fused_computation.16 | convolution fusion | flops 137361408 | bytes 7610624 | tf_op jit(solution)/shard_map/qhd,swhd->hqsw/dot_general | solution.py:154
  115.9 2.4 %select_reduce_fusion.1 = (f32[16,128]{1,0:T(8,128)}, f32[16,128]{1,0:T(8,128)S(1)}, f32[16,128,2,256]{3,1,2,0:T(8,128)S(1)}) fusion(f32[16,128,2,256]{3,1,2,0:T(8,128)S(1)} %get-tuple-element.62, f32[16,128]{1,0:T(8,128)S(1)} %get-tuple-element.61, pred[128,2]{0,1:T(4,128)(4,1)S(1)} %iota_compare_fusion.10, f32[16,128,256]{2,1,0:T(8,128)S(1)} %copy-done.15, ...), kind=kOutput, calls=%fused_computation.13 | convolution fusion | flops 141553664 | bytes 11821312 | tf_op jit(solution)/shard_map/qhd,swhd->hqsw/dot_general | solution.py:154
  118.4 2.0 copy-done.2
  120.3 1.2 select_reduce_fusion
  121.5 5.3 %copy.101 = f32[16,128,2,256]{1,3,2,0:T(8,128)} copy(f32[16,128,2,256]{3,1,2,0:T(8,128)} %copy-done.2) | data formatting | bytes 8388608 | tf_op jit(solution)/shard_map/add | solution.py:157
  126.9 5.3 %copy.95 = f32[16,128,2,256]{1,3,2,0:T(8,128)} copy(f32[16,128,2,256]{3,1,2,0:T(8,128)} %copy-done.1) | data formatting | bytes 8388608 | tf_op jit(solution)/shard_map/add | solution.py:157
  132.2 4.9 %copy.96 = bf16[2,256,1024]{1,0,2:T(2,128)(2,1)} copy(bf16[2,256,1024]{2,0,1:T(2,128)(2,1)} %get-tuple-element.26) | data formatting | bytes 2097152 | tf_op jit(solution)/shard_map/slice | solution.py:152
  137.1 2.6 %reshape.536 = bf16[512,16,64]{0,2,1:T(8,128)(2,1)} reshape(bf16[2,256,1024]{1,0,2:T(2,128)(2,1)} %copy.96) | data formatting | bytes 2097152 | tf_op jit(solution)/shard_map/reshape | solution.py:152
  139.7 4.9 %copy.102 = bf16[2,256,1024]{1,0,2:T(2,128)(2,1)} copy(bf16[2,256,1024]{2,0,1:T(2,128)(2,1)} %get-tuple-element.24) | data formatting | bytes 2097152 | tf_op jit(solution)/shard_map/slice | solution.py:152
  144.5 2.6 %reshape.539 = bf16[512,16,64]{0,2,1:T(8,128)(2,1)} reshape(bf16[2,256,1024]{1,0,2:T(2,128)(2,1)} %copy.102) | data formatting | bytes 2097152 | tf_op jit(solution)/shard_map/reshape | solution.py:152
  147.1 0.7 fusion.94
  147.8 1.6 fusion.31
  149.4 0.3 fusion.30
  149.7 5.3 %fusion.4 = (bf16[16,128,512]{1,2,0:T(8,128)(2,1)S(1)}, bf16[16,128,512]{1,2,0:T(8,128)(2,1)S(1)}) fusion(f32[16,128,2,256]{1,3,2,0:T(8,128)} %copy.101, f32[16,128]{1,0:T(8,128)S(1)} %get-tuple-element.12, pred[128,512]{0,1:T(8,128)(4,1)S(1)} %bitcast.222, f32[16,128]{1,0:T(8,128)S(1)} %get-tuple-element.61, f32[16,128,2,256]{1,3,2,0:T(8,128)} %copy.95), kind=kLoop, calls=%fused_computation.6 | loop fusion | flops 8388608 | bytes 12664832 | tf_op jit(solution)/shard_map/convert_element_type | solution.py:77
  155.1 0.5 fusion.21
  155.6 0.7 copy-done.11
  156.3 0.5 fusion.22
  156.9 0.7 copy-done.8
  157.6 0.3 fusion.32
  157.9 0.7 copy-done.14
  158.6 0.5 multiply_reduce_fusion
  159.2 0.8 multiply_convert_fusion
  160.1 15.1 %all-gather.5.cloned.1.call-done = bf16[512,1024]{1,0:T(8,128)(2,1)} async-done(((bf16[128,1024]{1,0:T(8,128)(2,1)}), bf16[512,1024]{1,0:T(8,128)(2,1)}) %all-gather.5.cloned.1.call-update) | async-done | bytes 1048592 | tf_op jit(solution)/shard_map/all_gather | solution.py:194
  175.2 5.3 %convolution_convert_fusion = bf16[512,1024]{1,0:T(8,128)(2,1)} fusion(bf16[1024,1024]{1,0:T(8,128)(2,1)S(1)} %copy-done, bf16[512,1024]{1,0:T(8,128)(2,1)} %all-gather.5.cloned.1.call-done, bf16[1024,1024]{1,0:T(8,128)(2,1)} %param.24), kind=kOutput, calls=%fused_computation.27 | convolution fusion | flops 2149056512 | bytes 6291456 | tf_op jit(solution)/shard_map/dot_general | solution.py:98
  180.5 25.0 %reduce-scatter.2.cloned.1.call-done = bf16[128,1024]{1,0:T(8,128)(2,1)} async-done(((bf16[512,1024]{1,0:T(8,128)(2,1)}), bf16[128,1024]{1,0:T(8,128)(2,1)}) %reduce-scatter.2.cloned.1.call-update) | async-done | bytes 262160 | tf_op jit(solution)/shard_map/reduce_scatter | solution.py:195
  205.5 1.7 add_convert_fusion
  (78 shorter events, 1.7 us)
Async XLA Ops:
  6.5 168.6 %copy-start = (bf16[1024,1024]{1,0:T(8,128)(2,1)S(1)}, bf16[1024,1024]{1,0:T(8,128)(2,1)}, u32[]{:S(2)}) copy-start(bf16[1024,1024]{1,0:T(8,128)(2,1)} %param.25) | copy-start | bytes 6291460
  6.5 6.1 %copy-start.4 = (bf16[128,1024]{1,0:T(8,128)(2,1)S(1)}, bf16[128,1024]{1,0:T(8,128)(2,1)}, u32[]{:S(2)}) copy-start(bf16[128,1024]{1,0:T(8,128)(2,1)} %param.13) | copy-start | bytes 786436
  6.5 6.1 %copy-start.21 = (f32[1024]{0:T(1024)S(1)}, f32[1024]{0:T(1024)}, u32[]{:S(2)}) copy-start(f32[1024]{0:T(1024)} %param.14) | copy-start | bytes 12292
  6.5 93.5 %all-gather.3.cloned.1.call-start = ((), (), s32[]{:S(2)}) async-start(), calls=%async_computation.1 | async-start | bytes 4718592 | tf_op jit(solution)/shard_map/all_gather | solution.py:143
  9.1 166.1 %all-gather.5.cloned.1.call-start = ((), (), s32[]{:S(2)}) async-start(), calls=%async_computation.2 | async-start | bytes 1310720 | tf_op jit(solution)/shard_map/all_gather | solution.py:194
  9.2 3.5 %copy-start.13 = (bf16[1024,1024]{1,0:T(8,128)(2,1)S(1)}, bf16[1024,1024]{1,0:T(8,128)(2,1)}, u32[]{:S(2)}) copy-start(bf16[1024,1024]{1,0:T(8,128)(2,1)} %param.16) | copy-start | bytes 6291460
  12.7 0.7 copy-start.12
  14.2 10.8 %copy-start.25 = (s32[1,16]{1,0:T(1,128)S(1)}, s32[1,16]{1,0:T(1,128)}, u32[]{:S(2)}) copy-start(s32[1,16]{1,0:T(1,128)} %param.21) | copy-start | bytes 196
  14.2 12.0 %copy-start.20 = (f32[32,16]{0,1:T(8,128)S(1)}, f32[32,16]{0,1:T(8,128)}, u32[]{:S(2)}) copy-start(f32[32,16]{0,1:T(8,128)} %param.19) | copy-start | bytes 6148
  14.2 41.6 %collective-permute-start.1 = (bf16[128,2048]{1,0:T(8,128)(2,1)}, bf16[128,2048]{1,0:T(8,128)(2,1)}, u32[]{:S(2)}, u32[]{:S(2)}) collective-permute-start(bf16[128,2048]{1,0:T(8,128)(2,1)} %pad_maximum_fusion), channel_id=1, source_target_pairs={{1,0},{2,1},{3,2},{4,3},{5,4},{6,5},{7,6},{9,8},{10,9},{11,10},{12... | collective-permute-start | bytes 1572872 | tf_op jit(solution)/shard_map/ppermute | solution.py:26
  15.6 45.7 %collective-permute-start = (bf16[128,2048]{1,0:T(8,128)(2,1)}, bf16[128,2048]{1,0:T(8,128)(2,1)}, u32[]{:S(2)}, u32[]{:S(2)}) collective-permute-start(bf16[128,2048]{1,0:T(8,128)(2,1)} %pad_maximum_fusion), channel_id=1, source_target_pairs={{0,1},{1,2},{2,3},{3,4},{4,5},{5,6},{6,7},{8,9},{9,10},{10,11},{11... | collective-permute-start | bytes 1572872 | tf_op jit(solution)/shard_map/ppermute | solution.py:25
  24.8 3.7 %copy-start.26 = (s32[1,16]{1,0:T(1,128)S(1)}, s32[1,16]{1,0:T(1,128)}, u32[]{:S(2)}) copy-start(s32[1,16]{1,0:T(1,128)} %param.22) | copy-start | bytes 196
  28.4 3.3 %copy-start.9 = (f32[128,128,16]{0,1,2:T(8,128)S(1)}, f32[128,128,16]{0,1,2:T(8,128)}, u32[]{:S(2)}) copy-start(f32[128,128,16]{0,1,2:T(8,128)} %copy.109) | copy-start | bytes 3145732
  55.8 62.5 %copy-start.22 = (pred[128,2]{0,1:T(4,128)(4,1)}, pred[128,2]{0,1:T(4,128)(4,1)S(1)}, u32[]{:S(2)}) copy-start(pred[128,2]{0,1:T(4,128)(4,1)S(1)} %iota_compare_fusion.10) | copy-start | bytes 772
  66.8 3.2 %copy-start.10 = (f32[128,128,16]{0,1,2:T(8,128)S(1)}, f32[128,128,16]{0,1,2:T(8,128)}, u32[]{:S(2)}) copy-start(f32[128,128,16]{0,1,2:T(8,128)} %copy.105) | copy-start | bytes 3145732
  66.8 3.2 %copy-start.17 = (bf16[128,1024]{0,1:T(8,128)(2,1)S(1)}, bf16[128,1024]{0,1:T(8,128)(2,1)}, u32[]{:S(2)}) copy-start(bf16[128,1024]{0,1:T(8,128)(2,1)} %copy.104) | copy-start | bytes 786436
  68.7 1.0 copy-start.3
  70.3 1.1 copy-start.7
  113.0 2.9 %copy-start.15 = (f32[16,128,256]{2,1,0:T(8,128)S(1)}, f32[16,128,256]{2,1,0:T(8,128)}, u32[]{:S(2)}) copy-start(f32[16,128,256]{2,1,0:T(8,128)} %copy.100) | copy-start | bytes 6291460
  113.0 2.9 %copy-start.18 = (bf16[2,256,1024]{1,2,0:T(8,128)(2,1)S(1)}, bf16[2,256,1024]{1,2,0:T(8,128)(2,1)}, u32[]{:S(2)}) copy-start(bf16[2,256,1024]{1,2,0:T(8,128)(2,1)} %copy.123) | copy-start | bytes 3145732
  115.9 2.5 %copy-start.1 = (f32[16,128,2,256]{3,1,2,0:T(8,128)}, f32[16,128,2,256]{3,1,2,0:T(8,128)S(1)}, u32[]{:S(2)}) copy-start(f32[16,128,2,256]{3,1,2,0:T(8,128)S(1)} %get-tuple-element.62) | copy-start | bytes 12582916
  118.3 2.0 copy-start.2
  144.5 4.9 %copy-start.16 = (bf16[128,1024]{0,1:T(8,128)(2,1)S(1)}, bf16[128,1024]{0,1:T(8,128)(2,1)}, u32[]{:S(2)}) copy-start(bf16[128,1024]{0,1:T(8,128)(2,1)} %copy.110) | copy-start | bytes 786436
  147.1 2.6 %copy-start.23 = (pred[128,2]{0,1:T(4,128)(4,1)S(1)}, pred[128,2]{0,1:T(4,128)(4,1)}, u32[]{:S(2)}) copy-start(pred[128,2]{0,1:T(4,128)(4,1)} %copy-done.22) | copy-start | bytes 772
  149.7 5.4 %copy-start.6 = (bf16[512,16,64]{0,2,1:T(8,128)(2,1)S(1)}, bf16[512,16,64]{0,2,1:T(8,128)(2,1)}, u32[]{:S(2)}) copy-start(bf16[512,16,64]{0,2,1:T(8,128)(2,1)} %reshape.536) | copy-start | bytes 3145732
  155.1 1.2 copy-start.11
  156.3 1.2 copy-start.8
  156.3 1.3 copy-start.19
  156.8 1.1 copy-start.5
  156.9 1.8 copy-start.14
  157.9 1.3 copy-start.24
  160.0 45.5 %reduce-scatter.2.cloned.1.call-start = ((), (), s32[]{:S(2)}) async-start(), calls=%async_computation.3 | async-start | bytes 1310720 | tf_op jit(solution)/shard_map/reduce_scatter | solution.py:195
Sparse Core Ops, SparseCore 0:
  9.5 90.4 all-gather.2
  160.2 14.9 all-gather.4
  180.6 24.8 reduce-scatter.1
where the time goes:
time: 215 us; the launch traced here: 214 us
  local copies, waits for them, and re-layouts  78.8 us (37%)
  waiting for transfers between devices  68.6 us (32%)
  matrix products  30.9 us (14%)
  other arithmetic  14.2 us (7%)
  between operations  13.5 us (6%)
  starting transfers between devices  7.77 us (4%)
    all_gather x1, waiting for transfers between devices, body(): shard_kv = lax.all_gather(prefix_cache, 'req', axis=1, tiled=True)  28.4 us
    reduce_scatter x1, waiting for transfers between devices, body(): lax.psum_scatter(feed_forward(gathered, w_in, w_out).astype(jnp.bfloat16)...  25 us
    unnamed x57, local copies, waits for them, and re-layouts  16.2 us
    slice x3, local copies, waits for them, and re-layouts, body(): value_rows = block[:, :, D:].reshape(-1, H, DK)  15.4 us
    all_gather x1, waiting for transfers between devices, body(): gathered = lax.all_gather(normed_two, 'grp', axis=0, tiled=True)  15.1 us
    dynamic_slice x3, local copies, waits for them, and re-layouts, body(): rel_terms = lax.dynamic_slice_in_dim(prefix_bias, begin, width, 2)  11 us
    add x2, local copies, waits for them, and re-layouts, body(): prefix_scores + rel_terms[:, :, None, :]  10.6 us
    dot_general x4, matrix products, bias_lookup(): jnp.einsum('qkb,bh->hqk', one_hot, rel_bias, precision=lax.Precision.HIGH...  8.1 us
  transfers between devices with their start and end apart: 5, of which 3 were waited for; matrix products, arithmetic and copies ran while one was open for 24% of the time, Pallas kernels for 0%

commit v1 on v0

--- a/solution.py
+++ b/solution.py
@@ -1,6 +1,10 @@
+import functools
+
 import jax
 import jax.numpy as jnp
 from jax import lax
+from jax.experimental import pallas as pl
+from jax.experimental.pallas import tpu as pltpu
 from jax.sharding import PartitionSpec as P
 
 D = 1024
@@ -8,6 +12,8 @@
 DK = 64
 PLEN = 512
 PREF_GRP = 2
+LANES = 128
+MESH = pl.DeviceIdType.MESH
 
 
 epsilon = 1e-06
@@ -201,9 +207,521 @@
     return (hidden_one.astype(jnp.float32) + mlp_total).astype(jnp.bfloat16)
 
 
+def bucket_steps():
+    return tuple((i, i) for i in range(1, 9)) + tuple((t, 9 + i) for i, t in enumerate(far_marks))
+
+
+def chain(distance, table, head, first):
+    value = jnp.full(distance.shape, table[first, head], jnp.float32)
+    for threshold, number in bucket_steps():
+        value = jnp.where(distance >= threshold, table[first + number, head], value)
+    return value
+
+
+def layer_kernel(
+    n_req,
+    tokens_hbm,
+    attn_gain,
+    wq_hbm,
+    wk_hbm,
+    wv_hbm,
+    wo_hbm,
+    rel_bias,
+    cache_hbm,
+    lengths,
+    prefix_map,
+    mlp_gain,
+    win_hbm,
+    wout_hbm,
+    out_ref,
+    tok,
+    w_attn,
+    w_in,
+    w_out,
+    normed,
+    stage,
+    k_cache,
+    v_cache,
+    q_all,
+    kv_all,
+    tail_bias,
+    near_bias,
+    key_req,
+    row_prefix,
+    row_max,
+    row_sum,
+    row_acc,
+    o_send,
+    att,
+    h_one,
+    n_two,
+    units,
+    part_own,
+    part_far,
+    fast_out,
+    fast_in,
+    chip_out,
+    chip_in,
+    far_out,
+    far_in,
+    load_sem,
+    own_sem,
+    kc_send,
+    kc_recv,
+    vc_send,
+    vc_recv,
+    q_send,
+    q_recv,
+    kv_send,
+    kv_recv,
+    o_ssem,
+    o_rsem,
+    f_send,
+    f_recv,
+):
+    me = lax.axis_index("req")
+    grp = lax.axis_index("grp")
+    side = lax.rem(grp, 2)
+    plane = lax.div(grp, 2)
+    mate = plane * 2 + (1 - side)
+    across = (1 - plane) * 2 + side
+    rows = tokens_hbm.shape[0]
+    piece = cache_hbm.shape[1]
+    half = rows // 2
+
+    def remote(src, dst, ssem, rsem, **where):
+        return pltpu.make_async_remote_copy(
+            src_ref=src, dst_ref=dst, send_sem=ssem, recv_sem=rsem, device_id=where, device_id_type=MESH
+        )
+
+    def lanes_of(index):
+        return pl.ds(pl.multiple_of(index * LANES, LANES), LANES)
+
+    def rows_of(index):
+        return pl.ds(pl.multiple_of(index * rows, rows), rows)
+
+    loads = [
+        pltpu.make_async_copy(src, dst, load_sem.at[i])
+        for i, (src, dst) in enumerate(
+            [
+                (tokens_hbm, tok),
+                (wq_hbm, w_attn.at[0]),
+                (wk_hbm, w_attn.at[1]),
+                (wv_hbm, w_attn.at[2]),
+                (wo_hbm, w_attn.at[3]),
+                (win_hbm, w_in),
+                (wout_hbm, w_out),
+            ]
+        )
+    ]
+    for load in loads:
+        load.start()
+
+    barrier = pltpu.get_barrier_semaphore()
+    for d in range(1, n_req):
+        pl.semaphore_signal(
+            barrier, inc=1, device_id={"req": lax.rem(me + d, n_req)}, device_id_type=MESH
+        )
+    for other in (mate, across):
+        pl.semaphore_signal(barrier, inc=1, device_id={"grp": other}, device_id_type=MESH)
+    pl.semaphore_wait(barrier, n_req + 1)
+
+    def cache_copy(buf, first, sends, recvs, d, peer, owner):
+        return remote(
+            cache_hbm.at[:, :, pl.ds(pl.multiple_of(first + peer * LANES, LANES), LANES)],
+            buf.at[:, pl.ds(pl.multiple_of(owner * piece, piece), piece), :],
+            sends.at[d],
+            recvs.at[d],
+            req=peer,
+        )
+
+    def q_copy(d, peer, owner):
+        return remote(
+            stage.at[0, :, lanes_of(peer)], q_all.at[rows_of(owner), :], q_send.at[d], q_recv.at[d], req=peer
+        )
+
+    def kv_copy(d, peer, owner):
+        return remote(
+            stage.at[pl.ds(1, 2), :, lanes_of(peer)],
+            kv_all.at[:, rows_of(owner + 1), :],
+            kv_send.at[d],
+            kv_recv.at[d],
+            req=peer,
+        )
+
+    def o_copy(d, peer, owner):
+        return remote(
+            o_send.at[peer], att.at[:, lanes_of(owner)], o_ssem.at[d], o_rsem.at[d], req=peer
+        )
+
+    def outgoing(make):
+        return [make(d, lax.rem(me + d, n_req), me) for d in range(1, n_req)]
+
+    def incoming(make):
+        return [
+            make(d, lax.rem(me + d, n_req), lax.rem(me + n_req - d, n_req)) for d in range(1, n_req)
+        ]
+
+    def kc_copy(d, peer, owner):
+        return cache_copy(k_cache, 0, kc_send, kc_recv, d, peer, owner)
+
+    def vc_copy(d, peer, owner):
+        return cache_copy(v_cache, D, vc_send, vc_recv, d, peer, owner)
+
+    for copy in outgoing(kc_copy) + outgoing(vc_copy):
+        copy.start()
+    own_copies = [
+        pltpu.make_async_copy(
+            cache_hbm.at[:, :, pl.ds(pl.multiple_of(first + me * LANES, LANES), LANES)],
+            buf.at[:, pl.ds(pl.multiple_of(me * piece, piece), piece), :],
+            own_sem.at[i],
+        )
+        for i, (buf, first) in enumerate([(k_cache, 0), (v_cache, D)])
+    ]
+    for copy in own_copies:
+        copy.start()
+
+    loads[0].wait()
+    wide = tok[...].astype(jnp.float32)
+    scale = lax.rsqrt(jnp.mean(wide * wide, axis=-1, keepdims=True) + epsilon)
+    normed[...] = (wide * scale * attn_gain[...]).astype(jnp.bfloat16)
+
+    tile = 256
+    for part in range(3):
+        loads[1 + part].wait()
+
+        @pl.loop(0, D // tile)
+        def _(t, part=part):
+            cols = pl.ds(pl.multiple_of(t * tile, tile), tile)
+            stage[part, :, cols] = jnp.dot(
+                normed[...], w_attn[part, :, cols], preferred_element_type=jnp.float32
+            ).astype(jnp.bfloat16)
+
+        if part == 0:
+            for copy in outgoing(q_copy):
+                copy.start()
+        if part == 2:
+            for copy in outgoing(kv_copy):
+                copy.start()
+    q_all[rows_of(me), :] = stage[0, :, lanes_of(me)]
+    zeros = jnp.zeros((rows, LANES), jnp.bfloat16)
+    for part in range(2):
+        kv_all[part, rows_of(me + 1), :] = stage[1 + part, :, lanes_of(me)]
+        kv_all[part, pl.ds(0, rows), :] = zeros
+        kv_all[part, pl.ds((n_req + 1) * rows, rows), :] = zeros
+
+    ends = []
+    total = 0
+    n_requests = lengths.shape[1]
+    for j in range(n_requests):
+        total = total + lengths[0, j]
+        ends.append(total)
+    key_ids = lax.broadcasted_iota(jnp.int32, key_req.shape, 1) - rows
+    key_number = jnp.where(key_ids < 0, -1, 0)
+    for end in ends:
+        key_number = key_number + jnp.where(key_ids >= end, 1, 0)
+    key_req[...] = key_number
+
+    row_iota = lax.broadcasted_iota(jnp.int32, (rows, LANES), 0)
+    lane_iota = lax.broadcasted_iota(jnp.int32, (rows, LANES), 1)
+    for head in range(2):
+        for part in range(3):
+            ahead = lane_iota + (part - 1) * rows - row_iota
+            distance = jnp.abs(ahead)
+            before = chain(distance, rel_bias, 2 * me + head, 0)
+            after = chain(distance, rel_bias, 2 * me + head, 16)
+            near_bias[0, pl.ds(head * rows, rows), pl.ds(part * LANES, LANES)] = jnp.where(
+                ahead > 0, after, before
+            )
+
+    @pl.loop(0, n_req)
+    def _(step):
+        b = n_req - 1 - step
+        ids = row_iota + b * rows
+        number = jnp.zeros_like(ids)
+        start = jnp.zeros_like(ids)
+        prefix = jnp.full(ids.shape, prefix_map[0, 0], jnp.int32)
+        for j in range(n_requests):
+            past = ids >= ends[j]
+            number = number + jnp.where(past, 1, 0)
+            start = start + jnp.where(past, lengths[0, j], 0)
+            if j + 1 < n_requests:
+                prefix = jnp.where(past, prefix_map[0, j + 1], prefix)
+        row_prefix[b] = prefix
+        distance = LANES + ids - start - lane_iota
+        for head in range(2):
+            tail_bias[b, pl.ds(head * rows, rows), :] = chain(distance, rel_bias, 2 * me + head, 0)
+        for part in range(3):
+            other = key_req[pl.ds(0, 1), pl.ds(pl.multiple_of(b * rows + part * LANES, LANES), LANES)]
+            same = other == number
+            for head in range(2):
+                here = (pl.ds(head * rows, rows), pl.ds(part * LANES, LANES))
+                near_bias[b, here[0], here[1]] = jnp.where(
+                    same, near_bias[0, here[0], here[1]], masked_score
+                )
+
+    first_head = lane_iota < DK
+
+    def query_heads(b):
+        q = q_all[rows_of(b), :]
+        nothing = jnp.zeros_like(q)
+        return jnp.concatenate(
+            [jnp.where(first_head, q, nothing), jnp.where(first_head, nothing, q)], axis=0
+        )
+
+    for copy in own_copies:
+        copy.wait()
+    for make in (kc_copy, q_copy, vc_copy):
+        for copy in incoming(make):
+            copy.wait_recv()
+
+    far_bias = jnp.concatenate(
+        [jnp.full((rows, 1), rel_bias[15, 2 * me + head], jnp.float32) for head in range(2)], axis=0
+    )
+    far_keys = PLEN - LANES
+
+    @pl.loop(0, n_req)
+    def _(b):
+        qh = query_heads(b)
+        choice = row_prefix[b]
+        zero_first = jnp.concatenate([choice, choice], axis=0) == 0
+        nothing = jnp.zeros_like(qh)
+        q2 = jnp.concatenate(
+            [jnp.where(zero_first, qh, nothing), jnp.where(zero_first, nothing, qh)], axis=1
+        )
+        keys = jnp.concatenate([k_cache[0], k_cache[1]], axis=1)
+        scores = lax.dot_general(
+            q2, keys, (((1,), (1,)), ((), ())), preferred_element_type=jnp.float32
+        )
+        scores = jnp.concatenate(
+            [scores[:, :far_keys] + far_bias, scores[:, far_keys:] + tail_bias[b]], axis=1
+        )
+        top = jnp.max(scores, axis=1, keepdims=True)
+        terms = jnp.exp(scores - top)
+        row_max[b] = jnp.broadcast_to(top, (2 * rows, LANES))
+        row_sum[b] = jnp.broadcast_to(jnp.sum(terms, axis=1, keepdims=True), (2 * rows, LANES))
+        values = jnp.concatenate([v_cache[0], v_cache[1]], axis=1)
+        acc = jnp.dot(terms.astype(jnp.bfloat16), values, preferred_element_type=jnp.float32)
+        row_acc[b] = jnp.where(zero_first, acc[:, :LANES], acc[:, LANES:])
+
+    for copy in incoming(kv_copy):
+        copy.wait_recv()
+
+    def near(b):
+        qh = query_heads(b)
+        window = pl.ds(pl.multiple_of(b * rows, rows), 3 * rows)
+        scores = (
+            lax.dot_general(
+                qh,
+                kv_all[0, window, :],
+                (((1,), (1,)), ((), ())),
+                preferred_element_type=jnp.float32,
+            )
+            + near_bias[b]
+        )
+        old = row_max[b]
+        top = jnp.maximum(old, jnp.max(scores, axis=1, keepdims=True))
+        terms = jnp.exp(scores - jnp.concatenate([top, top, top], axis=1))
+        shrink = jnp.exp(old - top)
+        denom = row_sum[b] * shrink + jnp.sum(terms, axis=1, keepdims=True)
+        acc = row_acc[b] * shrink + jnp.dot(
+            terms.astype(jnp.bfloat16), kv_all[1, window, :], preferred_element_type=jnp.float32
+        )
+        result = acc / denom
+        return jnp.where(first_head, result[:rows], result[rows:]).astype(jnp.bfloat16)
+
+    @pl.loop(1, n_req)
+    def _(d):
+        b = lax.rem(me + d, n_req)
+        o_send[b] = near(b)
+        o_copy(d, b, me).start()
+
+    att[:, lanes_of(me)] = near(me)
+
+    loads[4].wait()
+    for copy in incoming(o_copy):
+        copy.wait_recv()
+
+    @pl.loop(0, D // tile)
+    def _(t):
+        cols = pl.ds(pl.multiple_of(t * tile, tile), tile)
+        h_one[:, cols] = (
+            tok[:, cols].astype(jnp.float32)
+            + jnp.dot(att[...], w_attn[3, :, cols], preferred_element_type=jnp.float32)
+        ).astype(jnp.bfloat16)
+
+    wide = h_one[...].astype(jnp.float32)
+    scale = lax.rsqrt(jnp.mean(wide * wide, axis=-1, keepdims=True) + epsilon)
+    n_two[0] = (wide * scale * mlp_gain[...]).astype(jnp.bfloat16)
+
+    mine = remote(n_two.at[0], n_two.at[1], f_send.at[0], f_recv.at[0], grp=mate)
+    parts = [pl.ds(r * half, half) for r in range(2)]
+    cross = [
+        remote(n_two.at[0, parts[r]], n_two.at[2, parts[r]], f_send.at[1 + r], f_recv.at[1 + r], grp=across)
+        for r in range(2)
+    ]
+    relay = [
+        remote(n_two.at[2, parts[r]], n_two.at[3, parts[r]], f_send.at[3 + r], f_recv.at[3 + r], grp=mate)
+        for r in range(2)
+    ]
+    back = remote(fast_out, fast_in, f_send.at[5], f_recv.at[5], grp=mate)
+    swap = [
+        remote(chip_out.at[r], chip_in.at[r], f_send.at[6 + r], f_recv.at[6 + r], grp=mate) for r in range(2)
+    ]
+    home = [
+        remote(far_out.at[r], far_in.at[r], f_send.at[8 + r], f_recv.at[8 + r], grp=across) for r in range(2)
+    ]
+    for copy in cross:
+        copy.start()
+    mine.start()
+    loads[5].wait()
+    loads[6].wait()
+
+    def feed(rows_in, count, out):
+        @pl.loop(0, w_in.shape[0] // tile)
+        def _(t):
+            cols = pl.ds(pl.multiple_of(t * tile, tile), tile)
+            units[pl.ds(0, count), cols] = jnp.maximum(
+                lax.dot_general(
+                    rows_in,
+                    w_in[cols, :],
+                    (((1,), (1,)), ((), ())),
+                    preferred_element_type=jnp.float32,
+                ),
+                0.0,
+            ).astype(jnp.bfloat16)
+
+        @pl.loop(0, D // tile)
+        def _(t):
+            cols = pl.ds(pl.multiple_of(t * tile, tile), tile)
+            out[pl.ds(0, count), cols] = jnp.dot(
+                units[pl.ds(0, count), :], w_out[:, cols], preferred_element_type=jnp.float32
+            )
+
+    mine.wait_recv()
+    feed(jnp.concatenate([n_two[0], n_two[1]], axis=0), 2 * rows, part_own)
+    fast_out[...] = part_own[pl.ds(rows, rows), :].astype(jnp.bfloat16)
+    back.start()
+    for r in range(2):
+        cross[r].wait_recv()
+        relay[r].start()
+    for r in range(2):
+        relay[r].wait_recv()
+        feed(jnp.concatenate([n_two[2, parts[r]], n_two[3, parts[r]]], axis=0), rows, part_far)
+        chip_out[r] = part_far[pl.ds(half, half), :].astype(jnp.bfloat16)
+        swap[r].start()
+        swap[r].wait_recv()
+        far_out[r] = (part_far[pl.ds(0, half), :] + chip_in[r].astype(jnp.float32)).astype(jnp.bfloat16)
+        home[r].start()
+    back.wait_recv()
+    for r in range(2):
+        home[r].wait_recv()
+        out_ref[parts[r], :] = (
+            h_one[parts[r], :].astype(jnp.float32)
+            + part_own[parts[r], :]
+            + fast_in[parts[r], :].astype(jnp.float32)
+            + far_in[r].astype(jnp.float32)
+        ).astype(jnp.bfloat16)
+
+    for make in (kc_copy, vc_copy, q_copy, kv_copy, o_copy):
+        for copy in outgoing(make):
+            copy.wait_send()
+    for copy in [mine, back] + cross + relay + swap + home:
+        copy.wait_send()
+
+
+def fused(
+    tokens,
+    attn_gain,
+    w_query,
+    w_key,
+    w_value,
+    w_attn_out,
+    rel_bias,
+    prefix_cache,
+    lengths,
+    prefix_map,
+    mlp_gain,
+    w_in,
+    w_out,
+):
+    n_req = lax.axis_size("req")
+    rows = tokens.shape[0]
+    group = n_req * rows
+    hbm = pl.BlockSpec(memory_space=pl.ANY)
+    vmem = pl.BlockSpec(memory_space=pltpu.VMEM)
+    smem = pl.BlockSpec(memory_space=pltpu.SMEM)
+    half = rows // 2
+    bf16, f32 = jnp.bfloat16, jnp.float32
+    sems = pltpu.SemaphoreType.DMA
+    return pl.pallas_call(
+        functools.partial(layer_kernel, n_req),
+        out_shape=jax.ShapeDtypeStruct((rows, D), bf16),
+        in_specs=[hbm, vmem, hbm, hbm, hbm, hbm, smem, hbm, smem, smem, vmem, hbm, hbm],
+        out_specs=vmem,
+        scratch_shapes=[
+            pltpu.VMEM((rows, D), bf16),
+            pltpu.VMEM((4, D, D), bf16),
+            pltpu.VMEM(w_in.shape, bf16),
+            pltpu.VMEM(w_out.shape, bf16),
+            pltpu.VMEM((rows, D), bf16),
+            pltpu.VMEM((3, rows, D), bf16),
+            pltpu.VMEM((PREF_GRP, PLEN, LANES), bf16),
+            pltpu.VMEM((PREF_GRP, PLEN, LANES), bf16),
+            pltpu.VMEM((group, LANES), bf16),
+            pltpu.VMEM((2, group + 2 * rows, LANES), bf16),
+            pltpu.VMEM((n_req, 2 * rows, LANES), f32),
+            pltpu.VMEM((n_req, 2 * rows, 3 * LANES), f32),
+            pltpu.VMEM((8, group + 2 * rows), jnp.int32),
+            pltpu.VMEM((n_req, rows, LANES), jnp.int32),
+            pltpu.VMEM((n_req, 2 * rows, LANES), f32),
+            pltpu.VMEM((n_req, 2 * rows, LANES), f32),
+            pltpu.VMEM((n_req, 2 * rows, LANES), f32),
+            pltpu.VMEM((n_req, rows, LANES), bf16),
+            pltpu.VMEM((rows, D), bf16),
+            pltpu.VMEM((rows, D), bf16),
+            pltpu.VMEM((4, rows, D), bf16),
+            pltpu.VMEM((2 * rows, w_in.shape[0]), bf16),
+            pltpu.VMEM((2 * rows, D), f32),
+            pltpu.VMEM((rows, D), f32),
+            pltpu.VMEM((rows, D), bf16),
+            pltpu.VMEM((rows, D), bf16),
+            pltpu.VMEM((2, half, D), bf16),
+            pltpu.VMEM((2, half, D), bf16),
+            pltpu.VMEM((2, half, D), bf16),
+            pltpu.VMEM((2, half, D), bf16),
+            sems((7,)),
+            sems((2,)),
+        ]
+        + [sems((n_req,)) for _ in range(10)]
+        + [sems((10,)), sems((10,))],
+        compiler_params=pltpu.CompilerParams(
+            collective_id=0, has_side_effects=True, vmem_limit_bytes=48 * 1024 * 1024
+        ),
+    )(
+        tokens,
+        attn_gain.reshape(1, D),
+        w_query,
+        w_key,
+        w_value,
+        w_attn_out,
+        rel_bias,
+        prefix_cache,
+        lengths,
+        prefix_map,
+        mlp_gain.reshape(1, D),
+        w_in,
+        w_out,
+    )
+
+
+def pairs_fit(mesh):
+    return mesh.shape["req"] * LANES == D and mesh.shape["grp"] == 4
+
+
 def solution(mesh):
     return jax.shard_map(
-        body,
+        fused if pairs_fit(mesh) else body,
         mesh=mesh,
         in_specs=(
             P(("grp", "req"), None),

time: 215 us -> 72.1 us (0.34)
  local copies, waits for them, and re-layouts: 78.8 us -> 9.33 us
  waiting for transfers between devices: 68.6 us -> 0 us
  Pallas kernels: 0 us -> 62.4 us
  matrix products: 30.9 us -> 0 us
  other arithmetic: 14.2 us -> 0 us
  between operations: 13.5 us -> 0.02 us
  starting transfers between devices: 7.77 us -> 0 us
    pallas_call x0 -> x1, Pallas kernels: none -> 62.4 us  [fused(): pl.pallas_call(functools.partial(layer_kernel, n_req), out_shape=jax.Shap...]
    all_gather x2 -> x0, waiting for transfers between devices: 43.5 us -> none  [the longest x1 28.4 us: body(): shard_kv = lax.all_gather(prefix_cache, 'req', axis=1, tiled=True)]
    dot_general x19 -> x0, matrix products: 30.9 us -> none  [the longest x4 8.1 us: bias_lookup(): jnp.einsum('qkb,bh->hqk', one_hot, rel_bias, precision=lax.Precision.HIGH...]
    slice x11 -> x0, local copies, waits for them, and re-layouts: 26.4 us -> none  [the longest x3 15.4 us: body(): value_rows = block[:, :, D:].reshape(-1, H, DK)]
    reduce_scatter x1 -> x0, waiting for transfers between devices: 25 us -> none  [body(): lax.psum_scatter(feed_forward(gathered, w_in, w_out).astype(jnp.bfloat16)...]
    dynamic_slice x3 -> x0, local copies, waits for them, and re-layouts: 11 us -> none  [body(): rel_terms = lax.dynamic_slice_in_dim(prefix_bias, begin, width, 2)]
    add x2 -> x0, local copies, waits for them, and re-layouts: 10.6 us -> none  [body(): prefix_scores + rel_terms[:, :, None, :]]
    convert_element_type x3 -> x0, other arithmetic: 7.87 us -> none  [the longest x1 5.34 us: softmax_part(): exp_terms.astype(jnp.bfloat16)]
  transfers between devices with their start and end apart: 5 -> 0, of which waited for: 3 -> 0; matrix products, arithmetic and copies ran while one was open for 24% -> 0% of each run, Pallas kernels for 0% -> 0%
where the time goes in v1:
time: 72.1 us; the launch traced here: 71.8 us
  Pallas kernels  62.4 us (87%)
  local copies, waits for them, and re-layouts  9.33 us (13%)
    pallas_call x1, Pallas kernels, fused(): pl.pallas_call(functools.partial(layer_kernel, n_req), out_shape=jax.Shap...  62.4 us
    unnamed x18, local copies, waits for them, and re-layouts  9.33 us

profile of v1, /device:TPU:0, one launch (start us, length us, event | category | flops | bytes accessed | tf_op | source)
XLA Modules:
  0.0 71.8 jit_solution(11181145474870639115)
XLA Ops:
  0.0 0.8 %copy.14.rel_bias = f32[32,16]{1,0:T(8,128)S(1)} copy(f32[32,16]{0,1:T(8,128)} %param.19) | data formatting | bytes 4096 | tf_op args[6]
  0.8 0.0 copy-start
  0.8 1.6 %copy-done = bf16[1024,1024]{1,0:T(8,128)(2,1)S(1)} copy-done((bf16[1024,1024]{1,0:T(8,128)(2,1)S(1)}, bf16[1024,1024]{1,0:T(8,128)(2,1)}, u32[]{:S(2)}) %copy-start) | copy-done | bytes 2097176
  2.4 0.0 copy-start.1
  2.4 1.6 %copy-done.1 = bf16[1024,1024]{1,0:T(8,128)(2,1)S(1)} copy-done((bf16[1024,1024]{1,0:T(8,128)(2,1)S(1)}, bf16[1024,1024]{1,0:T(8,128)(2,1)}, u32[]{:S(2)}) %copy-start.1) | copy-done | bytes 2097176
  4.0 0.0 copy-start.2
  4.0 1.0 %copy-done.2 = bf16[2,64,2048]{2,1,0:T(8,128)(2,1)S(1)} copy-done((bf16[2,64,2048]{2,1,0:T(8,128)(2,1)S(1)}, bf16[2,64,2048]{2,1,0:T(8,128)(2,1)}, u32[]{:S(2)}) %copy-start.2) | copy-done | bytes 524312
  5.0 0.0 copy-start.3
  5.0 0.9 %copy-done.3 = bf16[128,1024]{1,0:T(8,128)(2,1)S(1)} copy-done((bf16[128,1024]{1,0:T(8,128)(2,1)S(1)}, bf16[128,1024]{1,0:T(8,128)(2,1)}, u32[]{:S(2)}) %copy-start.3) | copy-done | bytes 262168
  5.9 0.0 copy-start.4
  6.0 0.7 copy-done.4
  6.6 0.0 copy-start.5
  6.6 0.7 copy-done.5
  7.3 0.0 copy-start.6
  7.3 0.7 copy-done.6
  8.0 0.0 copy-start.7
  8.0 0.7 copy-done.7
  8.6 62.4 %shard_map.127 = bf16[128,1024]{1,0:T(8,128)(2,1)S(1)} custom-call(bf16[128,1024]{1,0:T(8,128)(2,1)S(1)} %copy-done.3, f32[1,1024]{1,0:T(1,128)S(1)} %bitcast.2, bf16[1024,1024]{1,0:T(8,128)(2,1)S(1)} %copy-done, bf16[1024,1024]{1,0:T(8,128)(2,1)S(1)} %copy-done.1, bf16[1024,1024]{1,0:T(8,128)(2,1)} %wv_hbm.1, bf16[1024,1024]{1,0:T(8,128)(2,1)} %wo_hbm.1, ...), custom_call_target="tpu_custom_call" | custom-call | tf_op jit(solution)/shard_map/pallas_call | solution.py:657
  71.1 0.7 copy.16
Async XLA Ops:
  0.8 1.6 %copy-start = (bf16[1024,1024]{1,0:T(8,128)(2,1)S(1)}, bf16[1024,1024]{1,0:T(8,128)(2,1)}, u32[]{:S(2)}) copy-start(bf16[1024,1024]{1,0:T(8,128)(2,1)} %wq_hbm.1) | copy-start | bytes 6291460
  2.4 1.6 %copy-start.1 = (bf16[1024,1024]{1,0:T(8,128)(2,1)S(1)}, bf16[1024,1024]{1,0:T(8,128)(2,1)}, u32[]{:S(2)}) copy-start(bf16[1024,1024]{1,0:T(8,128)(2,1)} %wk_hbm.1) | copy-start | bytes 6291460
  4.0 1.0 %copy-start.2 = (bf16[2,64,2048]{2,1,0:T(8,128)(2,1)S(1)}, bf16[2,64,2048]{2,1,0:T(8,128)(2,1)}, u32[]{:S(2)}) copy-start(bf16[2,64,2048]{2,1,0:T(8,128)(2,1)} %cache_hbm.1) | copy-start | bytes 1572868
  5.0 0.9 %copy-start.3 = (bf16[128,1024]{1,0:T(8,128)(2,1)S(1)}, bf16[128,1024]{1,0:T(8,128)(2,1)}, u32[]{:S(2)}) copy-start(bf16[128,1024]{1,0:T(8,128)(2,1)} %tokens_hbm.1) | copy-start | bytes 786436
  5.9 0.7 copy-start.4
  6.6 0.7 copy-start.5
  7.3 0.7 copy-start.6
  8.0 0.7 copy-start.7

commit v2 on v1

--- a/solution.py
+++ b/solution.py
@@ -212,9 +212,9 @@
 
 
 def chain(distance, table, head, first):
-    value = jnp.full(distance.shape, table[first, head], jnp.float32)
+    value = jnp.full(distance.shape, table[head, first], jnp.float32)
     for threshold, number in bucket_steps():
-        value = jnp.where(distance >= threshold, table[first + number, head], value)
+        value = jnp.where(distance >= threshold, table[head, first + number], value)
     return value
 
 
@@ -314,7 +314,7 @@
             ]
         )
     ]
-    for load in loads:
+    for load in loads[:4]:
         load.start()
 
     barrier = pltpu.get_barrier_semaphore()
@@ -349,10 +349,19 @@
             req=peer,
         )
 
-    def o_copy(d, peer, owner):
-        return remote(
-            o_send.at[peer], att.at[:, lanes_of(owner)], o_ssem.at[d], o_rsem.at[d], req=peer
-        )
+    parts = [pl.ds(r * half, half) for r in range(2)]
+
+    def o_copy(r):
+        def make(d, peer, owner):
+            return remote(
+                o_send.at[peer, parts[r]],
+                att.at[parts[r], lanes_of(owner)],
+                o_ssem.at[r, d],
+                o_rsem.at[r, d],
+                req=peer,
+            )
+
+        return make
 
     def outgoing(make):
         return [make(d, lax.rem(me + d, n_req), me) for d in range(1, n_req)]
@@ -400,6 +409,8 @@
         if part == 0:
             for copy in outgoing(q_copy):
                 copy.start()
+            for load in loads[4:]:
+                load.start()
         if part == 2:
             for copy in outgoing(kv_copy):
                 copy.start()
@@ -422,6 +433,9 @@
         key_number = key_number + jnp.where(key_ids >= end, 1, 0)
     key_req[...] = key_number
 
+    def stacked(r, head):
+        return pl.ds((2 * r + head) * half, half)
+
     row_iota = lax.broadcasted_iota(jnp.int32, (rows, LANES), 0)
     lane_iota = lax.broadcasted_iota(jnp.int32, (rows, LANES), 1)
     for head in range(2):
@@ -430,9 +444,9 @@
             distance = jnp.abs(ahead)
             before = chain(distance, rel_bias, 2 * me + head, 0)
             after = chain(distance, rel_bias, 2 * me + head, 16)
-            near_bias[0, pl.ds(head * rows, rows), pl.ds(part * LANES, LANES)] = jnp.where(
-                ahead > 0, after, before
-            )
+            both = jnp.where(ahead > 0, after, before)
+            for r in range(2):
+                near_bias[0, stacked(r, head), pl.ds(part * LANES, LANES)] = both[r * half : (r + 1) * half]
 
     @pl.loop(0, n_req)
     def _(step):
@@ -450,23 +464,28 @@
         row_prefix[b] = prefix
         distance = LANES + ids - start - lane_iota
         for head in range(2):
-            tail_bias[b, pl.ds(head * rows, rows), :] = chain(distance, rel_bias, 2 * me + head, 0)
+            terms = chain(distance, rel_bias, 2 * me + head, 0)
+            for r in range(2):
+                tail_bias[b, stacked(r, head), :] = terms[r * half : (r + 1) * half]
         for part in range(3):
             other = key_req[pl.ds(0, 1), pl.ds(pl.multiple_of(b * rows + part * LANES, LANES), LANES)]
             same = other == number
-            for head in range(2):
-                here = (pl.ds(head * rows, rows), pl.ds(part * LANES, LANES))
-                near_bias[b, here[0], here[1]] = jnp.where(
-                    same, near_bias[0, here[0], here[1]], masked_score
-                )
+            cols = pl.ds(part * LANES, LANES)
+            for r in range(2):
+                same_half = same[r * half : (r + 1) * half]
+                for head in range(2):
+                    near_bias[b, stacked(r, head), cols] = jnp.where(
+                        same_half, near_bias[0, stacked(r, head), cols], masked_score
+                    )
 
     first_head = lane_iota < DK
 
-    def query_heads(b):
-        q = q_all[rows_of(b), :]
+    def query_heads(b, r):
+        q = q_all[pl.ds(pl.multiple_of(b * rows + r * half, half), half), :]
         nothing = jnp.zeros_like(q)
+        first = first_head[:half]
         return jnp.concatenate(
-            [jnp.where(first_head, q, nothing), jnp.where(first_head, nothing, q)], axis=0
+            [jnp.where(first, q, nothing), jnp.where(first, nothing, q)], axis=0
         )
 
     for copy in own_copies:
@@ -476,15 +495,17 @@
             copy.wait_recv()
 
     far_bias = jnp.concatenate(
-        [jnp.full((rows, 1), rel_bias[15, 2 * me + head], jnp.float32) for head in range(2)], axis=0
+        [jnp.full((half, 1), rel_bias[2 * me + head, 15], jnp.float32) for head in range(2)] * 2, axis=0
     )
     far_keys = PLEN - LANES
 
     @pl.loop(0, n_req)
     def _(b):
-        qh = query_heads(b)
+        qh = jnp.concatenate([query_heads(b, 0), query_heads(b, 1)], axis=0)
         choice = row_prefix[b]
-        zero_first = jnp.concatenate([choice, choice], axis=0) == 0
+        zero_first = jnp.concatenate(
+            [choice[:half], choice[:half], choice[half:], choice[half:]], axis=0
+        ) == 0
         nothing = jnp.zeros_like(qh)
         q2 = jnp.concatenate(
             [jnp.where(zero_first, qh, nothing), jnp.where(zero_first, nothing, qh)], axis=1
@@ -507,9 +528,10 @@
     for copy in incoming(kv_copy):
         copy.wait_recv()
 
-    def near(b):
-        qh = query_heads(b)
+    def near(b, r):
+        qh = query_heads(b, r)
         window = pl.ds(pl.multiple_of(b * rows, rows), 3 * rows)
+        here = pl.ds(r * rows, rows)
         scores = (
             lax.dot_general(
                 qh,
@@ -517,45 +539,33 @@
                 (((1,), (1,)), ((), ())),
                 preferred_element_type=jnp.float32,
             )
-            + near_bias[b]
-        )
-        old = row_max[b]
+            + near_bias[b, here, :]
+        )
+        old = row_max[b, here, :]
         top = jnp.maximum(old, jnp.max(scores, axis=1, keepdims=True))
         terms = jnp.exp(scores - jnp.concatenate([top, top, top], axis=1))
         shrink = jnp.exp(old - top)
-        denom = row_sum[b] * shrink + jnp.sum(terms, axis=1, keepdims=True)
-        acc = row_acc[b] * shrink + jnp.dot(
+        denom = row_sum[b, here, :] * shrink + jnp.sum(terms, axis=1, keepdims=True)
+        acc = row_acc[b, here, :] * shrink + jnp.dot(
             terms.astype(jnp.bfloat16), kv_all[1, window, :], preferred_element_type=jnp.float32
         )
         result = acc / denom
-        return jnp.where(first_head, result[:rows], result[rows:]).astype(jnp.bfloat16)
-
-    @pl.loop(1, n_req)
-    def _(d):
-        b = lax.rem(me + d, n_req)
-        o_send[b] = near(b)
-        o_copy(d, b, me).start()
-
-    att[:, lanes_of(me)] = near(me)
-
-    loads[4].wait()
-    for copy in incoming(o_copy):
-        copy.wait_recv()
-
-    @pl.loop(0, D // tile)
-    def _(t):
-        cols = pl.ds(pl.multiple_of(t * tile, tile), tile)
-        h_one[:, cols] = (
-            tok[:, cols].astype(jnp.float32)
-            + jnp.dot(att[...], w_attn[3, :, cols], preferred_element_type=jnp.float32)
-        ).astype(jnp.bfloat16)
-
-    wide = h_one[...].astype(jnp.float32)
-    scale = lax.rsqrt(jnp.mean(wide * wide, axis=-1, keepdims=True) + epsilon)
-    n_two[0] = (wide * scale * mlp_gain[...]).astype(jnp.bfloat16)
-
-    mine = remote(n_two.at[0], n_two.at[1], f_send.at[0], f_recv.at[0], grp=mate)
-    parts = [pl.ds(r * half, half) for r in range(2)]
+        return jnp.where(first_head[:half], result[:half], result[half:]).astype(jnp.bfloat16)
+
+    for r in range(2):
+
+        @pl.loop(1, n_req)
+        def _(d, r=r):
+            b = lax.rem(me + d, n_req)
+            o_send[b, parts[r], :] = near(b, r)
+            o_copy(r)(d, b, me).start()
+
+        att[parts[r], lanes_of(me)] = near(me, r)
+
+    mine = [
+        remote(n_two.at[0, parts[r]], n_two.at[1, parts[r]], f_send.at[10 + r], f_recv.at[10 + r], grp=mate)
+        for r in range(2)
+    ]
     cross = [
         remote(n_two.at[0, parts[r]], n_two.at[2, parts[r]], f_send.at[1 + r], f_recv.at[1 + r], grp=across)
         for r in range(2)
@@ -571,17 +581,36 @@
     home = [
         remote(far_out.at[r], far_in.at[r], f_send.at[8 + r], f_recv.at[8 + r], grp=across) for r in range(2)
     ]
-    for copy in cross:
-        copy.start()
-    mine.start()
+
+    loads[4].wait()
+    for r in range(2):
+        for copy in incoming(o_copy(r)):
+            copy.wait_recv()
+
+        @pl.loop(0, D // tile)
+        def _(t, r=r):
+            cols = pl.ds(pl.multiple_of(t * tile, tile), tile)
+            h_one[parts[r], cols] = (
+                tok[parts[r], cols].astype(jnp.float32)
+                + jnp.dot(
+                    att[parts[r], :], w_attn[3, :, cols], preferred_element_type=jnp.float32
+                )
+            ).astype(jnp.bfloat16)
+
+        wide = h_one[parts[r], :].astype(jnp.float32)
+        scale = lax.rsqrt(jnp.mean(wide * wide, axis=-1, keepdims=True) + epsilon)
+        n_two[0, parts[r], :] = (wide * scale * mlp_gain[...]).astype(jnp.bfloat16)
+        cross[r].start()
+        mine[r].start()
+
     loads[5].wait()
     loads[6].wait()
 
-    def feed(rows_in, count, out):
+    def up(rows_in):
         @pl.loop(0, w_in.shape[0] // tile)
         def _(t):
             cols = pl.ds(pl.multiple_of(t * tile, tile), tile)
-            units[pl.ds(0, count), cols] = jnp.maximum(
+            units[:, cols] = jnp.maximum(
                 lax.dot_general(
                     rows_in,
                     w_in[cols, :],
@@ -591,42 +620,60 @@
                 0.0,
             ).astype(jnp.bfloat16)
 
+    def down(out):
         @pl.loop(0, D // tile)
         def _(t):
             cols = pl.ds(pl.multiple_of(t * tile, tile), tile)
-            out[pl.ds(0, count), cols] = jnp.dot(
-                units[pl.ds(0, count), :], w_out[:, cols], preferred_element_type=jnp.float32
-            )
-
-    mine.wait_recv()
-    feed(jnp.concatenate([n_two[0], n_two[1]], axis=0), 2 * rows, part_own)
-    fast_out[...] = part_own[pl.ds(rows, rows), :].astype(jnp.bfloat16)
+            out[:, cols] = jnp.dot(
+                units[...], w_out[:, cols], preferred_element_type=jnp.float32
+            ).astype(out.dtype)
+
+    def far_rows(r):
+        return jnp.concatenate([n_two[2, parts[r]], n_two[3, parts[r]]], axis=0)
+
+    def send_home(r):
+        swap[r].wait_recv()
+        far_out[r] = (part_far[r, pl.ds(0, half), :] + chip_in[r].astype(jnp.float32)).astype(jnp.bfloat16)
+        home[r].start()
+
+    def finish_far(r):
+        down(part_far.at[r])
+        chip_out[r] = part_far[r, pl.ds(half, half), :].astype(jnp.bfloat16)
+        swap[r].start()
+
+    up(n_two[0])
+    cross[0].wait_recv()
+    relay[0].start()
+    down(part_own)
+    for copy in mine:
+        copy.wait_recv()
+    up(n_two[1])
+    down(fast_out)
     back.start()
-    for r in range(2):
-        cross[r].wait_recv()
-        relay[r].start()
-    for r in range(2):
-        relay[r].wait_recv()
-        feed(jnp.concatenate([n_two[2, parts[r]], n_two[3, parts[r]]], axis=0), rows, part_far)
-        chip_out[r] = part_far[pl.ds(half, half), :].astype(jnp.bfloat16)
-        swap[r].start()
-        swap[r].wait_recv()
-        far_out[r] = (part_far[pl.ds(0, half), :] + chip_in[r].astype(jnp.float32)).astype(jnp.bfloat16)
-        home[r].start()
+    cross[1].wait_recv()
+    relay[1].start()
+    relay[0].wait_recv()
+    up(far_rows(0))
+    finish_far(0)
+    relay[1].wait_recv()
+    up(far_rows(1))
+    send_home(0)
+    finish_far(1)
     back.wait_recv()
+    part_own[...] = (
+        part_own[...] + h_one[...].astype(jnp.float32) + fast_in[...].astype(jnp.float32)
+    )
+    send_home(1)
     for r in range(2):
         home[r].wait_recv()
         out_ref[parts[r], :] = (
-            h_one[parts[r], :].astype(jnp.float32)
-            + part_own[parts[r], :]
-            + fast_in[parts[r], :].astype(jnp.float32)
-            + far_in[r].astype(jnp.float32)
+            part_own[parts[r], :] + far_in[r].astype(jnp.float32)
         ).astype(jnp.bfloat16)
 
-    for make in (kc_copy, vc_copy, q_copy, kv_copy, o_copy):
+    for make in (kc_copy, vc_copy, q_copy, kv_copy, o_copy(0), o_copy(1)):
         for copy in outgoing(make):
             copy.wait_send()
-    for copy in [mine, back] + cross + relay + swap + home:
+    for copy in [back] + mine + cross + relay + swap + home:
         copy.wait_send()
 
 
@@ -681,9 +728,9 @@
             pltpu.VMEM((rows, D), bf16),
             pltpu.VMEM((rows, D), bf16),
             pltpu.VMEM((4, rows, D), bf16),
-            pltpu.VMEM((2 * rows, w_in.shape[0]), bf16),
-            pltpu.VMEM((2 * rows, D), f32),
+            pltpu.VMEM((rows, w_in.shape[0]), bf16),
             pltpu.VMEM((rows, D), f32),
+            pltpu.VMEM((2, rows, D), f32),
             pltpu.VMEM((rows, D), bf16),
             pltpu.VMEM((rows, D), bf16),
             pltpu.VMEM((2, half, D), bf16),
@@ -693,10 +740,11 @@
             sems((7,)),
             sems((2,)),
         ]
-        + [sems((n_req,)) for _ in range(10)]
-        + [sems((10,)), sems((10,))],
+        + [sems((n_req,)) for _ in range(8)]
+        + [sems((2, n_req)) for _ in range(2)]
+        + [sems((12,)), sems((12,))],
         compiler_params=pltpu.CompilerParams(
-            collective_id=0, has_side_effects=True, vmem_limit_bytes=48 * 1024 * 1024
+            collective_id=0, has_side_effects=True, vmem_limit_bytes=63 * 1024 * 1024
         ),
     )(
         tokens,
@@ -705,7 +753,7 @@
         w_key,
         w_value,
         w_attn_out,
-        rel_bias,
+        rel_bias.T,
         prefix_cache,
         lengths,
         prefix_map,

time: 72.1 us -> 66.3 us (0.920)
  local copies, waits for them, and re-layouts: 9.33 us -> 1.67 us
  Pallas kernels: 62.4 us -> 64.4 us
    unnamed x18 -> x1, local copies, waits for them, and re-layouts: 9.33 us -> 1.67 us
    pallas_call x1, Pallas kernels: 62.4 us -> 64.4 us  [fused(): pl.pallas_call(functools.partial(layer_kernel, n_req), out_shape=jax.Shap...]
where the time goes in v2:
time: 66.3 us; the launch traced here: 66.1 us
  Pallas kernels  64.4 us (97%)
  local copies, waits for them, and re-layouts  1.67 us (3%)
    pallas_call x1, Pallas kernels, fused(): pl.pallas_call(functools.partial(layer_kernel, n_req), out_shape=jax.Shap...  64.4 us
    unnamed x1, local copies, waits for them, and re-layouts  1.67 us

profile of v2, /device:TPU:0, one launch (start us, length us, event | category | flops | bytes accessed | tf_op | source)
XLA Modules:
  0.0 66.1 jit_solution(3210398979213159887)
XLA Ops:
  0.0 64.4 %shard_map.127 = bf16[128,1024]{1,0:T(8,128)(2,1)} custom-call(bf16[128,1024]{1,0:T(8,128)(2,1)} %tokens_hbm.1, f32[1,1024]{1,0:T(1,128)} %bitcast.4, bf16[1024,1024]{1,0:T(8,128)(2,1)} %wq_hbm.1, bf16[1024,1024]{1,0:T(8,128)(2,1)} %wk_hbm.1, bf16[1024,1024]{1,0:T(8,128)(2,1)} %wv_hbm.1, bf16[1024,1024]{1,0:T(8,128)(2,1)} %wo_hbm.1, f32[16,32]{1,0:T(8,128)} %bitcast.3, ...), custom_call_target="tpu_custom_call" | custom-call | tf_op jit(solution)/shard_map/pallas_call | solution.py:704
  64.4 1.7 %copy.15 = bf16[128,1024]{1,0:T(8,128)(2,1)} copy(bf16[128,1024]{1,0:T(8,128)(2,1)} %shard_map.127) | data formatting | bytes 524288

commit v3 on v2

--- a/solution.py
+++ b/solution.py
@@ -243,7 +243,11 @@
     k_cache,
     v_cache,
     q_all,
-    kv_all,
+    k_side,
+    k_all,
+    v_all,
+    k_cross,
+    w_up,
     tail_bias,
     near_bias,
     key_req,
@@ -272,8 +276,10 @@
     vc_recv,
     q_send,
     q_recv,
-    kv_send,
-    kv_recv,
+    k_send,
+    k_recv,
+    v_send,
+    v_recv,
     o_ssem,
     o_rsem,
     f_send,
@@ -340,13 +346,14 @@
             stage.at[0, :, lanes_of(peer)], q_all.at[rows_of(owner), :], q_send.at[d], q_recv.at[d], req=peer
         )
 
-    def kv_copy(d, peer, owner):
+    def k_copy(d, peer, owner):
         return remote(
-            stage.at[pl.ds(1, 2), :, lanes_of(peer)],
-            kv_all.at[:, rows_of(owner + 1), :],
-            kv_send.at[d],
-            kv_recv.at[d],
-            req=peer,
+            k_side.at[lanes_of(peer), :], k_all.at[:, lanes_of(owner + 1)], k_send.at[d], k_recv.at[d], req=peer
+        )
+
+    def v_copy(d, peer, owner):
+        return remote(
+            stage.at[1, :, lanes_of(peer)], v_all.at[rows_of(owner + 1), :], v_send.at[d], v_recv.at[d], req=peer
         )
 
     parts = [pl.ds(r * half, half) for r in range(2)]
@@ -395,31 +402,34 @@
     scale = lax.rsqrt(jnp.mean(wide * wide, axis=-1, keepdims=True) + epsilon)
     normed[...] = (wide * scale * attn_gain[...]).astype(jnp.bfloat16)
 
-    tile = 256
+    tile = 512
+    makers = (q_copy, k_copy, v_copy)
     for part in range(3):
         loads[1 + part].wait()
 
         @pl.loop(0, D // tile)
         def _(t, part=part):
             cols = pl.ds(pl.multiple_of(t * tile, tile), tile)
-            stage[part, :, cols] = jnp.dot(
+            made = jnp.dot(
                 normed[...], w_attn[part, :, cols], preferred_element_type=jnp.float32
             ).astype(jnp.bfloat16)
-
+            if part == 1:
+                k_side[cols, :] = made.T
+            else:
+                stage[part // 2, :, cols] = made
+
+        for copy in outgoing(makers[part]):
+            copy.start()
         if part == 0:
-            for copy in outgoing(q_copy):
-                copy.start()
             for load in loads[4:]:
                 load.start()
-        if part == 2:
-            for copy in outgoing(kv_copy):
-                copy.start()
     q_all[rows_of(me), :] = stage[0, :, lanes_of(me)]
+    k_all[:, lanes_of(me + 1)] = k_side[lanes_of(me), :]
+    v_all[rows_of(me + 1), :] = stage[1, :, lanes_of(me)]
     zeros = jnp.zeros((rows, LANES), jnp.bfloat16)
-    for part in range(2):
-        kv_all[part, rows_of(me + 1), :] = stage[1 + part, :, lanes_of(me)]
-        kv_all[part, pl.ds(0, rows), :] = zeros
-        kv_all[part, pl.ds((n_req + 1) * rows, rows), :] = zeros
+    for outer in (0, n_req + 1):
+        k_all[:, pl.ds(outer * rows, rows)] = zeros
+        v_all[pl.ds(outer * rows, rows), :] = zeros
 
     ends = []
     total = 0
@@ -478,6 +488,13 @@
                         same_half, near_bias[0, stacked(r, head), cols], masked_score
                     )
 
+    loads[5].wait()
+
+    @pl.loop(0, w_in.shape[0] // tile)
+    def _(t):
+        cols = pl.ds(pl.multiple_of(t * tile, tile), tile)
+        w_up[:, cols] = w_in[cols, :].T
+
     first_head = lane_iota < DK
 
     def query_heads(b, r):
@@ -490,7 +507,11 @@
 
     for copy in own_copies:
         copy.wait()
-    for make in (kc_copy, q_copy, vc_copy):
+    for copy in incoming(kc_copy):
+        copy.wait_recv()
+    for which in range(PREF_GRP):
+        k_cross[pl.ds(which * LANES, LANES), :] = k_cache[which].T
+    for make in (q_copy, vc_copy):
         for copy in incoming(make):
             copy.wait_recv()
 
@@ -499,68 +520,82 @@
     )
     far_keys = PLEN - LANES
 
-    @pl.loop(0, n_req)
-    def _(b):
+    def far_scores(b):
         qh = jnp.concatenate([query_heads(b, 0), query_heads(b, 1)], axis=0)
         choice = row_prefix[b]
-        zero_first = jnp.concatenate(
-            [choice[:half], choice[:half], choice[half:], choice[half:]], axis=0
-        ) == 0
+        zero_first = (
+            jnp.concatenate([choice[:half], choice[:half], choice[half:], choice[half:]], axis=0) == 0
+        )
         nothing = jnp.zeros_like(qh)
         q2 = jnp.concatenate(
             [jnp.where(zero_first, qh, nothing), jnp.where(zero_first, nothing, qh)], axis=1
         )
-        keys = jnp.concatenate([k_cache[0], k_cache[1]], axis=1)
-        scores = lax.dot_general(
-            q2, keys, (((1,), (1,)), ((), ())), preferred_element_type=jnp.float32
-        )
+        scores = jnp.dot(q2, k_cross[...], preferred_element_type=jnp.float32)
         scores = jnp.concatenate(
             [scores[:, :far_keys] + far_bias, scores[:, far_keys:] + tail_bias[b]], axis=1
         )
+        return zero_first, scores
+
+    def far_terms(scores):
         top = jnp.max(scores, axis=1, keepdims=True)
         terms = jnp.exp(scores - top)
-        row_max[b] = jnp.broadcast_to(top, (2 * rows, LANES))
-        row_sum[b] = jnp.broadcast_to(jnp.sum(terms, axis=1, keepdims=True), (2 * rows, LANES))
+        return top, jnp.sum(terms, axis=1, keepdims=True), terms.astype(jnp.bfloat16)
+
+    far_step = 2
+
+    @pl.loop(0, n_req // far_step)
+    def _(step):
+        blocks = [step * far_step + i for i in range(far_step)]
         values = jnp.concatenate([v_cache[0], v_cache[1]], axis=1)
-        acc = jnp.dot(terms.astype(jnp.bfloat16), values, preferred_element_type=jnp.float32)
-        row_acc[b] = jnp.where(zero_first, acc[:, :LANES], acc[:, LANES:])
-
-    for copy in incoming(kv_copy):
-        copy.wait_recv()
-
-    def near(b, r):
-        qh = query_heads(b, r)
-        window = pl.ds(pl.multiple_of(b * rows, rows), 3 * rows)
+        scored = [far_scores(b) for b in blocks]
+        termed = [far_terms(scores) for _, scores in scored]
+        accs = [jnp.dot(t[2], values, preferred_element_type=jnp.float32) for t in termed]
+        for b, (zero_first, _), (top, total, _), acc in zip(blocks, scored, termed, accs):
+            row_max[b] = jnp.broadcast_to(top, (2 * rows, LANES))
+            row_sum[b] = jnp.broadcast_to(total, (2 * rows, LANES))
+            row_acc[b] = jnp.where(zero_first, acc[:, :LANES], acc[:, LANES:])
+
+    for make in (k_copy, v_copy):
+        for copy in incoming(make):
+            copy.wait_recv()
+
+    def near(blocks, r):
         here = pl.ds(r * rows, rows)
-        scores = (
-            lax.dot_general(
-                qh,
-                kv_all[0, window, :],
-                (((1,), (1,)), ((), ())),
-                preferred_element_type=jnp.float32,
-            )
+        windows = [pl.ds(pl.multiple_of(b * rows, rows), 3 * rows) for b in blocks]
+        scores = [
+            jnp.dot(query_heads(b, r), k_all[:, w], preferred_element_type=jnp.float32)
             + near_bias[b, here, :]
-        )
-        old = row_max[b, here, :]
-        top = jnp.maximum(old, jnp.max(scores, axis=1, keepdims=True))
-        terms = jnp.exp(scores - jnp.concatenate([top, top, top], axis=1))
-        shrink = jnp.exp(old - top)
-        denom = row_sum[b, here, :] * shrink + jnp.sum(terms, axis=1, keepdims=True)
-        acc = row_acc[b, here, :] * shrink + jnp.dot(
-            terms.astype(jnp.bfloat16), kv_all[1, window, :], preferred_element_type=jnp.float32
-        )
-        result = acc / denom
-        return jnp.where(first_head[:half], result[:half], result[half:]).astype(jnp.bfloat16)
-
+            for b, w in zip(blocks, windows)
+        ]
+        olds = [row_max[b, here, :] for b in blocks]
+        tops = [jnp.maximum(o, jnp.max(x, axis=1, keepdims=True)) for o, x in zip(olds, scores)]
+        terms = [jnp.exp(x - jnp.concatenate([t, t, t], axis=1)) for x, t in zip(scores, tops)]
+        shrinks = [jnp.exp(o - t) for o, t in zip(olds, tops)]
+        sums = [
+            row_sum[b, here, :] * z + jnp.sum(x, axis=1, keepdims=True)
+            for b, z, x in zip(blocks, shrinks, terms)
+        ]
+        accs = [
+            row_acc[b, here, :] * z
+            + jnp.dot(x.astype(jnp.bfloat16), v_all[w, :], preferred_element_type=jnp.float32)
+            for b, z, x, w in zip(blocks, shrinks, terms, windows)
+        ]
+        results = [a / x for a, x in zip(accs, sums)]
+        return [jnp.where(first_head[:half], x[:half], x[half:]).astype(jnp.bfloat16) for x in results]
+
+    near_step = 4
     for r in range(2):
-
-        @pl.loop(1, n_req)
-        def _(d, r=r):
-            b = lax.rem(me + d, n_req)
-            o_send[b, parts[r], :] = near(b, r)
-            o_copy(r)(d, b, me).start()
-
-        att[parts[r], lanes_of(me)] = near(me, r)
+        for begin in range(1, n_req + 1, near_step):
+            turns = range(begin, begin + near_step)
+            blocks = [lax.rem(me + d, n_req) for d in turns]
+            for d, b, result in zip(turns, blocks, near(blocks, r)):
+                if d < n_req:
+                    o_send[b, parts[r], :] = result
+                else:
+                    att[parts[r], lanes_of(me)] = result
+            for d, b in zip(turns, blocks):
+                if d < n_req:
+                    o_copy(r)(d, b, me).start()
 
     mine = [
         remote(n_two.at[0, parts[r]], n_two.at[1, parts[r]], f_send.at[10 + r], f_recv.at[10 + r], grp=mate)
@@ -603,7 +638,6 @@
         cross[r].start()
         mine[r].start()
 
-    loads[5].wait()
     loads[6].wait()
 
     def up(rows_in):
@@ -611,13 +645,7 @@
         def _(t):
             cols = pl.ds(pl.multiple_of(t * tile, tile), tile)
             units[:, cols] = jnp.maximum(
-                lax.dot_general(
-                    rows_in,
-                    w_in[cols, :],
-                    (((1,), (1,)), ((), ())),
-                    preferred_element_type=jnp.float32,
-                ),
-                0.0,
+                jnp.dot(rows_in, w_up[:, cols], preferred_element_type=jnp.float32), 0.0
             ).astype(jnp.bfloat16)
 
     def down(out):
@@ -670,7 +698,7 @@
             part_own[parts[r], :] + far_in[r].astype(jnp.float32)
         ).astype(jnp.bfloat16)
 
-    for make in (kc_copy, vc_copy, q_copy, kv_copy, o_copy(0), o_copy(1)):
+    for make in (kc_copy, vc_copy, q_copy, k_copy, v_copy, o_copy(0), o_copy(1)):
         for copy in outgoing(make):
             copy.wait_send()
     for copy in [back] + mine + cross + relay + swap + home:
@@ -712,11 +740,15 @@
             pltpu.VMEM(w_in.shape, bf16),
             pltpu.VMEM(w_out.shape, bf16),
             pltpu.VMEM((rows, D), bf16),
-            pltpu.VMEM((3, rows, D), bf16),
+            pltpu.VMEM((2, rows, D), bf16),
             pltpu.VMEM((PREF_GRP, PLEN, LANES), bf16),
             pltpu.VMEM((PREF_GRP, PLEN, LANES), bf16),
             pltpu.VMEM((group, LANES), bf16),
-            pltpu.VMEM((2, group + 2 * rows, LANES), bf16),
+            pltpu.VMEM((D, rows), bf16),
+            pltpu.VMEM((LANES, group + 2 * rows), bf16),
+            pltpu.VMEM((group + 2 * rows, LANES), bf16),
+            pltpu.VMEM((PREF_GRP * LANES, PLEN), bf16),
+            pltpu.VMEM(w_in.shape[::-1], bf16),
             pltpu.VMEM((n_req, 2 * rows, LANES), f32),
             pltpu.VMEM((n_req, 2 * rows, 3 * LANES), f32),
             pltpu.VMEM((8, group + 2 * rows), jnp.int32),
@@ -740,7 +772,7 @@
             sems((7,)),
             sems((2,)),
         ]
-        + [sems((n_req,)) for _ in range(8)]
+        + [sems((n_req,)) for _ in range(10)]
         + [sems((2, n_req)) for _ in range(2)]
         + [sems((12,)), sems((12,))],
         compiler_params=pltpu.CompilerParams(

time: 66.3 us -> 63.1 us (0.952)
  Pallas kernels: 64.4 us -> 61.2 us
    pallas_call x1, Pallas kernels: 64.4 us -> 61.2 us  [fused(): pl.pallas_call(functools.partial(layer_kernel, n_req), out_shape=jax.Shap...]
where the time goes in v3:
time: 63.1 us; the launch traced here: 62.9 us
  Pallas kernels  61.2 us (97%)
  local copies, waits for them, and re-layouts  1.67 us (3%)
    pallas_call x1, Pallas kernels, fused(): pl.pallas_call(functools.partial(layer_kernel, n_req), out_shape=jax.Shap...  61.2 us
    unnamed x1, local copies, waits for them, and re-layouts  1.67 us

profile of v3, /device:TPU:0, one launch (start us, length us, event | category | flops | bytes accessed | tf_op | source)
XLA Modules:
  0.0 62.9 jit_solution(998705500568671981)
XLA Ops:
  0.0 61.2 %shard_map.127 = bf16[128,1024]{1,0:T(8,128)(2,1)} custom-call(bf16[128,1024]{1,0:T(8,128)(2,1)} %tokens_hbm.1, f32[1,1024]{1,0:T(1,128)} %bitcast.4, bf16[1024,1024]{1,0:T(8,128)(2,1)} %wq_hbm.1, bf16[1024,1024]{1,0:T(8,128)(2,1)} %wk_hbm.1, bf16[1024,1024]{1,0:T(8,128)(2,1)} %wv_hbm.1, bf16[1024,1024]{1,0:T(8,128)(2,1)} %wo_hbm.1, f32[16,32]{1,0:T(8,128)} %bitcast.3, ...), custom_call_target="tpu_custom_call" | custom-call | tf_op jit(solution)/shard_map/pallas_call | solution.py:732
  61.2 1.7 %copy.15 = bf16[128,1024]{1,0:T(8,128)(2,1)} copy(bf16[128,1024]{1,0:T(8,128)(2,1)} %shard_map.127) | data formatting | bytes 524288

commit v4 on v3

--- a/solution.py
+++ b/solution.py
@@ -243,19 +243,20 @@
     k_cache,
     v_cache,
     q_all,
-    k_side,
-    k_all,
-    v_all,
+    k_win,
+    v_win,
     k_cross,
     w_up,
     tail_bias,
     near_bias,
-    key_req,
     row_prefix,
     row_max,
     row_sum,
     row_acc,
     o_send,
+    l_send,
+    att_in,
+    l_in,
     att,
     h_one,
     n_two,
@@ -276,12 +277,12 @@
     vc_recv,
     q_send,
     q_recv,
-    k_send,
-    k_recv,
-    v_send,
-    v_recv,
+    n_send,
+    n_recv,
     o_ssem,
     o_rsem,
+    l_ssem,
+    l_rsem,
     f_send,
     f_recv,
 ):
@@ -343,18 +344,38 @@
 
     def q_copy(d, peer, owner):
         return remote(
-            stage.at[0, :, lanes_of(peer)], q_all.at[rows_of(owner), :], q_send.at[d], q_recv.at[d], req=peer
-        )
-
-    def k_copy(d, peer, owner):
-        return remote(
-            k_side.at[lanes_of(peer), :], k_all.at[:, lanes_of(owner + 1)], k_send.at[d], k_recv.at[d], req=peer
-        )
-
-    def v_copy(d, peer, owner):
-        return remote(
-            stage.at[1, :, lanes_of(peer)], v_all.at[rows_of(owner + 1), :], v_send.at[d], v_recv.at[d], req=peer
-        )
+            stage.at[:, lanes_of(peer)], q_all.at[rows_of(owner), :], q_send.at[d], q_recv.at[d], req=peer
+        )
+
+    odd = lax.rem(me, 2)
+    beside = me + 1 - 2 * odd
+    beyond = me - 1 + 2 * odd
+    onward = me + 2 - 4 * odd
+    has_beyond = jnp.logical_and(beyond >= 0, beyond < n_req)
+    has_onward = jnp.logical_and(onward >= 0, onward < n_req)
+    own_slot = pl.ds(rows, rows)
+
+    def slot(late):
+        return pl.ds(pl.multiple_of(2 * rows * late, LANES), rows)
+
+    k_beside = remote(k_win.at[:, own_slot], k_win.at[:, slot(odd)], n_send.at[0], n_recv.at[0], req=beside)
+    v_beside = remote(v_win.at[own_slot], v_win.at[slot(odd)], n_send.at[1], n_recv.at[1], req=beside)
+    k_beyond = remote(
+        k_win.at[:, own_slot], k_win.at[:, slot(1 - odd)], n_send.at[2], n_recv.at[2], req=beyond
+    )
+    v_onward = remote(
+        v_win.at[slot(1 - odd)], v_win.at[slot(odd)], n_send.at[3], n_recv.at[3], req=onward
+    )
+    k_beside_in = remote(
+        k_win.at[:, own_slot], k_win.at[:, slot(1 - odd)], n_send.at[0], n_recv.at[0], req=beside
+    )
+    v_beside_in = remote(v_win.at[own_slot], v_win.at[slot(1 - odd)], n_send.at[1], n_recv.at[1], req=beside)
+    k_beyond_in = remote(
+        k_win.at[:, own_slot], k_win.at[:, slot(odd)], n_send.at[2], n_recv.at[2], req=beyond
+    )
+    v_onward_in = remote(
+        v_win.at[own_slot], v_win.at[slot(odd)], n_send.at[3], n_recv.at[3], req=beyond
+    )
 
     parts = [pl.ds(r * half, half) for r in range(2)]
 
@@ -362,10 +383,18 @@
         def make(d, peer, owner):
             return remote(
                 o_send.at[peer, parts[r]],
-                att.at[parts[r], lanes_of(owner)],
+                att_in.at[parts[r], lanes_of(owner)],
                 o_ssem.at[r, d],
                 o_rsem.at[r, d],
                 req=peer,
+            )
+
+        return make
+
+    def l_copy(r):
+        def make(d, peer, owner):
+            return remote(
+                l_send.at[peer, r], l_in.at[owner, r], l_ssem.at[r, d], l_rsem.at[r, d], req=peer
             )
 
         return make
@@ -403,7 +432,6 @@
     normed[...] = (wide * scale * attn_gain[...]).astype(jnp.bfloat16)
 
     tile = 512
-    makers = (q_copy, k_copy, v_copy)
     for part in range(3):
         loads[1 + part].wait()
 
@@ -413,23 +441,32 @@
             made = jnp.dot(
                 normed[...], w_attn[part, :, cols], preferred_element_type=jnp.float32
             ).astype(jnp.bfloat16)
-            if part == 1:
-                k_side[cols, :] = made.T
+            if part == 0:
+                stage[:, cols] = made
+            elif part == 1:
+                k_win[cols, own_slot] = made.T
             else:
-                stage[part // 2, :, cols] = made
-
-        for copy in outgoing(makers[part]):
-            copy.start()
+                v_win[own_slot, cols] = made
+
         if part == 0:
+            for copy in outgoing(q_copy):
+                copy.start()
             for load in loads[4:]:
                 load.start()
-    q_all[rows_of(me), :] = stage[0, :, lanes_of(me)]
-    k_all[:, lanes_of(me + 1)] = k_side[lanes_of(me), :]
-    v_all[rows_of(me + 1), :] = stage[1, :, lanes_of(me)]
-    zeros = jnp.zeros((rows, LANES), jnp.bfloat16)
-    for outer in (0, n_req + 1):
-        k_all[:, pl.ds(outer * rows, rows)] = zeros
-        v_all[pl.ds(outer * rows, rows), :] = zeros
+        elif part == 1:
+            k_beside.start()
+
+            @pl.when(has_beyond)
+            def _():
+                k_beyond.start()
+        else:
+            v_beside.start()
+    q_all[rows_of(me), :] = stage[:, lanes_of(me)]
+
+    @pl.when(jnp.logical_not(has_beyond))
+    def _():
+        k_win[:, slot(odd)] = jnp.zeros((D, rows), jnp.bfloat16)
+        v_win[slot(odd), :] = jnp.zeros((rows, D), jnp.bfloat16)
 
     ends = []
     total = 0
@@ -437,37 +474,18 @@
     for j in range(n_requests):
         total = total + lengths[0, j]
         ends.append(total)
-    key_ids = lax.broadcasted_iota(jnp.int32, key_req.shape, 1) - rows
-    key_number = jnp.where(key_ids < 0, -1, 0)
-    for end in ends:
-        key_number = key_number + jnp.where(key_ids >= end, 1, 0)
-    key_req[...] = key_number
-
     def stacked(r, head):
         return pl.ds((2 * r + head) * half, half)
 
     row_iota = lax.broadcasted_iota(jnp.int32, (rows, LANES), 0)
     lane_iota = lax.broadcasted_iota(jnp.int32, (rows, LANES), 1)
-    for head in range(2):
-        for part in range(3):
-            ahead = lane_iota + (part - 1) * rows - row_iota
-            distance = jnp.abs(ahead)
-            before = chain(distance, rel_bias, 2 * me + head, 0)
-            after = chain(distance, rel_bias, 2 * me + head, 16)
-            both = jnp.where(ahead > 0, after, before)
-            for r in range(2):
-                near_bias[0, stacked(r, head), pl.ds(part * LANES, LANES)] = both[r * half : (r + 1) * half]
-
     @pl.loop(0, n_req)
-    def _(step):
-        b = n_req - 1 - step
+    def _(b):
         ids = row_iota + b * rows
-        number = jnp.zeros_like(ids)
         start = jnp.zeros_like(ids)
         prefix = jnp.full(ids.shape, prefix_map[0, 0], jnp.int32)
         for j in range(n_requests):
             past = ids >= ends[j]
-            number = number + jnp.where(past, 1, 0)
             start = start + jnp.where(past, lengths[0, j], 0)
             if j + 1 < n_requests:
                 prefix = jnp.where(past, prefix_map[0, j + 1], prefix)
@@ -477,16 +495,41 @@
             terms = chain(distance, rel_bias, 2 * me + head, 0)
             for r in range(2):
                 tail_bias[b, stacked(r, head), :] = terms[r * half : (r + 1) * half]
+
+    def request_of(ids):
+        number = jnp.where(ids < 0, -1, 0)
+        for end in ends:
+            number = number + jnp.where(ids >= end, 1, 0)
+        return number
+
+    own_number = request_of(row_iota + me * rows)
+    key_numbers = [
+        request_of(lax.broadcasted_iota(jnp.int32, (8, LANES), 1) + (me + part - 1) * rows)[:1]
+        for part in range(3)
+    ]
+
+    @pl.loop(0, n_req)
+    def _(pair):
         for part in range(3):
-            other = key_req[pl.ds(0, 1), pl.ds(pl.multiple_of(b * rows + part * LANES, LANES), LANES)]
-            same = other == number
-            cols = pl.ds(part * LANES, LANES)
-            for r in range(2):
-                same_half = same[r * half : (r + 1) * half]
-                for head in range(2):
-                    near_bias[b, stacked(r, head), cols] = jnp.where(
-                        same_half, near_bias[0, stacked(r, head), cols], masked_score
+            same = key_numbers[part] == own_number
+            ahead = lane_iota + (part - 1) * rows - row_iota
+            distance = jnp.abs(ahead)
+            for head in range(2):
+                if part == 0:
+                    both = chain(distance, rel_bias, 2 * pair + head, 0)
+                elif part == 2:
+                    both = chain(distance, rel_bias, 2 * pair + head, 16)
+                else:
+                    both = jnp.where(
+                        ahead > 0,
+                        chain(distance, rel_bias, 2 * pair + head, 16),
+                        chain(distance, rel_bias, 2 * pair + head, 0),
                     )
+                both = jnp.where(same, both, masked_score)
+                for r in range(2):
+                    near_bias[pair, stacked(r, head), pl.ds(part * LANES, LANES)] = both[
+                        r * half : (r + 1) * half
+                    ]
 
     loads[5].wait()
 
@@ -497,13 +540,21 @@
 
     first_head = lane_iota < DK
 
-    def query_heads(b, r):
-        q = q_all[pl.ds(pl.multiple_of(b * rows + r * half, half), half), :]
+    def query_heads(q):
         nothing = jnp.zeros_like(q)
         first = first_head[:half]
         return jnp.concatenate(
             [jnp.where(first, q, nothing), jnp.where(first, nothing, q)], axis=0
         )
+
+    def one_row(stack):
+        return jnp.where(first_head[:half], stack[:half], stack[half:]).astype(jnp.bfloat16)
+
+    v_beside_in.wait_recv()
+
+    @pl.when(has_onward)
+    def _():
+        v_onward.start()
 
     for copy in own_copies:
         copy.wait()
@@ -516,23 +567,22 @@
             copy.wait_recv()
 
     far_bias = jnp.concatenate(
-        [jnp.full((half, 1), rel_bias[2 * me + head, 15], jnp.float32) for head in range(2)] * 2, axis=0
+        [jnp.full((half, 1), rel_bias[2 * me + head, 15], jnp.float32) for head in range(2)], axis=0
     )
     far_keys = PLEN - LANES
 
-    def far_scores(b):
-        qh = jnp.concatenate([query_heads(b, 0), query_heads(b, 1)], axis=0)
-        choice = row_prefix[b]
-        zero_first = (
-            jnp.concatenate([choice[:half], choice[:half], choice[half:], choice[half:]], axis=0) == 0
-        )
+    def far_scores(b, r):
+        here = pl.ds(r * rows, rows)
+        qh = query_heads(q_all[pl.ds(pl.multiple_of(b * rows + r * half, half), half), :])
+        choice = row_prefix[b, parts[r], :]
+        zero_first = jnp.concatenate([choice, choice], axis=0) == 0
         nothing = jnp.zeros_like(qh)
         q2 = jnp.concatenate(
             [jnp.where(zero_first, qh, nothing), jnp.where(zero_first, nothing, qh)], axis=1
         )
         scores = jnp.dot(q2, k_cross[...], preferred_element_type=jnp.float32)
         scores = jnp.concatenate(
-            [scores[:, :far_keys] + far_bias, scores[:, far_keys:] + tail_bias[b]], axis=1
+            [scores[:, :far_keys] + far_bias, scores[:, far_keys:] + tail_bias[b, here, :]], axis=1
         )
         return zero_first, scores
 
@@ -541,61 +591,81 @@
         terms = jnp.exp(scores - top)
         return top, jnp.sum(terms, axis=1, keepdims=True), terms.astype(jnp.bfloat16)
 
-    far_step = 2
-
-    @pl.loop(0, n_req // far_step)
-    def _(step):
-        blocks = [step * far_step + i for i in range(far_step)]
+    def far(blocks, r):
         values = jnp.concatenate([v_cache[0], v_cache[1]], axis=1)
-        scored = [far_scores(b) for b in blocks]
+        scored = [far_scores(b, r) for b in blocks]
         termed = [far_terms(scores) for _, scores in scored]
         accs = [jnp.dot(t[2], values, preferred_element_type=jnp.float32) for t in termed]
-        for b, (zero_first, _), (top, total, _), acc in zip(blocks, scored, termed, accs):
-            row_max[b] = jnp.broadcast_to(top, (2 * rows, LANES))
-            row_sum[b] = jnp.broadcast_to(total, (2 * rows, LANES))
-            row_acc[b] = jnp.where(zero_first, acc[:, :LANES], acc[:, LANES:])
-
-    for make in (k_copy, v_copy):
-        for copy in incoming(make):
-            copy.wait_recv()
-
-    def near(blocks, r):
-        here = pl.ds(r * rows, rows)
-        windows = [pl.ds(pl.multiple_of(b * rows, rows), 3 * rows) for b in blocks]
-        scores = [
-            jnp.dot(query_heads(b, r), k_all[:, w], preferred_element_type=jnp.float32)
-            + near_bias[b, here, :]
-            for b, w in zip(blocks, windows)
-        ]
-        olds = [row_max[b, here, :] for b in blocks]
-        tops = [jnp.maximum(o, jnp.max(x, axis=1, keepdims=True)) for o, x in zip(olds, scores)]
-        terms = [jnp.exp(x - jnp.concatenate([t, t, t], axis=1)) for x, t in zip(scores, tops)]
-        shrinks = [jnp.exp(o - t) for o, t in zip(olds, tops)]
-        sums = [
-            row_sum[b, here, :] * z + jnp.sum(x, axis=1, keepdims=True)
-            for b, z, x in zip(blocks, shrinks, terms)
-        ]
-        accs = [
-            row_acc[b, here, :] * z
-            + jnp.dot(x.astype(jnp.bfloat16), v_all[w, :], preferred_element_type=jnp.float32)
-            for b, z, x, w in zip(blocks, shrinks, terms, windows)
-        ]
-        results = [a / x for a, x in zip(accs, sums)]
-        return [jnp.where(first_head[:half], x[:half], x[half:]).astype(jnp.bfloat16) for x in results]
-
-    near_step = 4
+        results = []
+        for (zero_first, _), (top, total, _), acc in zip(scored, termed, accs):
+            chosen = jnp.where(zero_first, acc[:, :LANES], acc[:, LANES:]) / total
+            logs = jnp.broadcast_to(top + jnp.log(total), (rows, LANES)).T
+            results.append((one_row(chosen), logs[:8]))
+        return results
+
+    far_step = 4
     for r in range(2):
-        for begin in range(1, n_req + 1, near_step):
-            turns = range(begin, begin + near_step)
+        for begin in range(1, n_req + 1, far_step):
+            turns = range(begin, begin + far_step)
             blocks = [lax.rem(me + d, n_req) for d in turns]
-            for d, b, result in zip(turns, blocks, near(blocks, r)):
+            for d, b, (result, logs) in zip(turns, blocks, far(blocks, r)):
                 if d < n_req:
                     o_send[b, parts[r], :] = result
+                    l_send[b, r] = logs
                 else:
-                    att[parts[r], lanes_of(me)] = result
+                    att_in[parts[r], lanes_of(me)] = result
+                    l_in[me, r] = logs
             for d, b in zip(turns, blocks):
                 if d < n_req:
                     o_copy(r)(d, b, me).start()
+                    l_copy(r)(d, b, me).start()
+
+    k_beside_in.wait_recv()
+
+    @pl.when(has_beyond)
+    def _():
+        k_beyond_in.wait_recv()
+        v_onward_in.wait_recv()
+
+    def near(pairs):
+        lanes = [lanes_of(pair) for pair in pairs]
+        scores = [
+            jnp.dot(
+                jnp.concatenate([query_heads(stage[parts[r], at]) for r in range(2)], axis=0),
+                k_win[at, :],
+                preferred_element_type=jnp.float32,
+            )
+            + near_bias[pair]
+            for pair, at in zip(pairs, lanes)
+        ]
+        tops = [jnp.max(x, axis=1, keepdims=True) for x in scores]
+        terms = [jnp.exp(x - t) for x, t in zip(scores, tops)]
+        accs = [
+            jnp.dot(x.astype(jnp.bfloat16), v_win[:, at], preferred_element_type=jnp.float32)
+            for x, at in zip(terms, lanes)
+        ]
+        for pair, top, x, acc in zip(pairs, tops, terms, accs):
+            row_max[pair] = jnp.broadcast_to(top, (2 * rows, LANES))
+            row_sum[pair] = jnp.broadcast_to(jnp.sum(x, axis=1, keepdims=True), (2 * rows, LANES))
+            row_acc[pair] = acc
+
+    near_step = 2
+
+    @pl.loop(0, n_req // near_step)
+    def _(step):
+        near([step * near_step + i for i in range(near_step)])
+
+    def merge(pair, r):
+        here = pl.ds(r * rows, rows)
+        at = pl.ds(pair * LANES, LANES)
+        logs = jnp.broadcast_to(l_in[pair, r, :1, :], (rows, LANES)).T
+        there = att_in[parts[r], at].astype(jnp.float32)
+        there = jnp.concatenate([there, there], axis=0)
+        top = jnp.maximum(logs, row_max[pair, here, :])
+        scale_one = jnp.exp(logs - top)
+        scale_two = jnp.exp(row_max[pair, here, :] - top)
+        whole = there * scale_one + row_acc[pair, here, :] * scale_two
+        att[parts[r], at] = one_row(whole / (scale_one + row_sum[pair, here, :] * scale_two))
 
     mine = [
         remote(n_two.at[0, parts[r]], n_two.at[1, parts[r]], f_send.at[10 + r], f_recv.at[10 + r], grp=mate)
@@ -619,8 +689,10 @@
 
     loads[4].wait()
     for r in range(2):
-        for copy in incoming(o_copy(r)):
+        for copy in incoming(o_copy(r)) + incoming(l_copy(r)):
             copy.wait_recv()
+        for pair in range(n_req):
+            merge(pair, r)
 
         @pl.loop(0, D // tile)
         def _(t, r=r):
@@ -698,7 +770,18 @@
             part_own[parts[r], :] + far_in[r].astype(jnp.float32)
         ).astype(jnp.bfloat16)
 
-    for make in (kc_copy, vc_copy, q_copy, k_copy, v_copy, o_copy(0), o_copy(1)):
+    k_beside.wait_send()
+    v_beside.wait_send()
+
+    @pl.when(has_beyond)
+    def _():
+        k_beyond.wait_send()
+
+    @pl.when(has_onward)
+    def _():
+        v_onward.wait_send()
+
+    for make in (kc_copy, vc_copy, q_copy, o_copy(0), o_copy(1), l_copy(0), l_copy(1)):
         for copy in outgoing(make):
             copy.wait_send()
     for copy in [back] + mine + cross + relay + swap + home:
@@ -740,23 +823,24 @@
             pltpu.VMEM(w_in.shape, bf16),
             pltpu.VMEM(w_out.shape, bf16),
             pltpu.VMEM((rows, D), bf16),
-            pltpu.VMEM((2, rows, D), bf16),
+            pltpu.VMEM((rows, D), bf16),
             pltpu.VMEM((PREF_GRP, PLEN, LANES), bf16),
             pltpu.VMEM((PREF_GRP, PLEN, LANES), bf16),
             pltpu.VMEM((group, LANES), bf16),
-            pltpu.VMEM((D, rows), bf16),
-            pltpu.VMEM((LANES, group + 2 * rows), bf16),
-            pltpu.VMEM((group + 2 * rows, LANES), bf16),
+            pltpu.VMEM((D, 3 * rows), bf16),
+            pltpu.VMEM((3 * rows, D), bf16),
             pltpu.VMEM((PREF_GRP * LANES, PLEN), bf16),
             pltpu.VMEM(w_in.shape[::-1], bf16),
             pltpu.VMEM((n_req, 2 * rows, LANES), f32),
             pltpu.VMEM((n_req, 2 * rows, 3 * LANES), f32),
-            pltpu.VMEM((8, group + 2 * rows), jnp.int32),
             pltpu.VMEM((n_req, rows, LANES), jnp.int32),
             pltpu.VMEM((n_req, 2 * rows, LANES), f32),
             pltpu.VMEM((n_req, 2 * rows, LANES), f32),
             pltpu.VMEM((n_req, 2 * rows, LANES), f32),
             pltpu.VMEM((n_req, rows, LANES), bf16),
+            pltpu.VMEM((n_req, 2, 8, LANES), f32),
+            pltpu.VMEM((rows, D), bf16),
+            pltpu.VMEM((n_req, 2, 8, LANES), f32),
             pltpu.VMEM((rows, D), bf16),
             pltpu.VMEM((rows, D), bf16),
             pltpu.VMEM((4, rows, D), bf16),
@@ -772,8 +856,9 @@
             sems((7,)),
             sems((2,)),
         ]
-        + [sems((n_req,)) for _ in range(10)]
-        + [sems((2, n_req)) for _ in range(2)]
+        + [sems((n_req,)) for _ in range(6)]
+        + [sems((4,)), sems((4,))]
+        + [sems((2, n_req)) for _ in range(4)]
         + [sems((12,)), sems((12,))],
         compiler_params=pltpu.CompilerParams(
             collective_id=0, has_side_effects=True, vmem_limit_bytes=63 * 1024 * 1024

time: 63.1 us -> 66.3 us (1.051)
  Pallas kernels: 61.2 us -> 64.4 us
    pallas_call x1, Pallas kernels: 61.2 us -> 64.4 us  [fused(): pl.pallas_call(functools.partial(layer_kernel, n_req), out_shape=jax.Shap...]
where the time goes in v4:
time: 66.3 us; the launch traced here: 66.1 us
  Pallas kernels  64.4 us (97%)
  local copies, waits for them, and re-layouts  1.67 us (3%)
    pallas_call x1, Pallas kernels, fused(): pl.pallas_call(functools.partial(layer_kernel, n_req), out_shape=jax.Shap...  64.4 us
    unnamed x1, local copies, waits for them, and re-layouts  1.67 us

profile of v4, /device:TPU:0, one launch (start us, length us, event | category | flops | bytes accessed | tf_op | source)
XLA Modules:
  0.0 66.1 jit_solution(2873612813967641685)
XLA Ops:
  0.0 64.4 %shard_map.127 = bf16[128,1024]{1,0:T(8,128)(2,1)} custom-call(bf16[128,1024]{1,0:T(8,128)(2,1)} %tokens_hbm.1, f32[1,1024]{1,0:T(1,128)} %bitcast.4, bf16[1024,1024]{1,0:T(8,128)(2,1)} %wq_hbm.1, bf16[1024,1024]{1,0:T(8,128)(2,1)} %wk_hbm.1, bf16[1024,1024]{1,0:T(8,128)(2,1)} %wv_hbm.1, bf16[1024,1024]{1,0:T(8,128)(2,1)} %wo_hbm.1, f32[16,32]{1,0:T(8,128)} %bitcast.3, ...), custom_call_target="tpu_custom_call" | custom-call | tf_op jit(solution)/shard_map/pallas_call | solution.py:815
  64.4 1.7 %copy.15 = bf16[128,1024]{1,0:T(8,128)(2,1)} copy(bf16[128,1024]{1,0:T(8,128)(2,1)} %shard_map.127) | data formatting | bytes 524288

commit v5 on v3

--- a/solution.py
+++ b/solution.py
@@ -251,7 +251,8 @@
     tail_bias,
     near_bias,
     key_req,
-    row_prefix,
+    row_facts,
+    row_code,
     row_max,
     row_sum,
     row_acc,
@@ -448,52 +449,32 @@
 
     row_iota = lax.broadcasted_iota(jnp.int32, (rows, LANES), 0)
     lane_iota = lax.broadcasted_iota(jnp.int32, (rows, LANES), 1)
-    for head in range(2):
-        for part in range(3):
-            ahead = lane_iota + (part - 1) * rows - row_iota
-            distance = jnp.abs(ahead)
-            before = chain(distance, rel_bias, 2 * me + head, 0)
-            after = chain(distance, rel_bias, 2 * me + head, 16)
-            both = jnp.where(ahead > 0, after, before)
-            for r in range(2):
-                near_bias[0, stacked(r, head), pl.ds(part * LANES, LANES)] = both[r * half : (r + 1) * half]
+    ids = lax.broadcasted_iota(jnp.int32, row_facts.shape, 0) * rows + lax.broadcasted_iota(
+        jnp.int32, row_facts.shape, 1
+    )
+    number = jnp.zeros_like(ids)
+    start = jnp.zeros_like(ids)
+    prefix = jnp.full(ids.shape, prefix_map[0, 0], jnp.int32)
+    for j in range(n_requests):
+        past = ids >= ends[j]
+        number = number + jnp.where(past, 1, 0)
+        start = start + jnp.where(past, lengths[0, j], 0)
+        if j + 1 < n_requests:
+            prefix = jnp.where(past, prefix_map[0, j + 1], prefix)
+    row_facts[...] = ((start * 2 + prefix) * 1024 + number).astype(jnp.float32)
+
+    def bias_of(distance, head, first):
+        return chain(distance, rel_bias, 2 * me + head, first) - rel_bias[2 * me + head, 15]
 
     @pl.loop(0, n_req)
-    def _(step):
-        b = n_req - 1 - step
-        ids = row_iota + b * rows
-        number = jnp.zeros_like(ids)
-        start = jnp.zeros_like(ids)
-        prefix = jnp.full(ids.shape, prefix_map[0, 0], jnp.int32)
-        for j in range(n_requests):
-            past = ids >= ends[j]
-            number = number + jnp.where(past, 1, 0)
-            start = start + jnp.where(past, lengths[0, j], 0)
-            if j + 1 < n_requests:
-                prefix = jnp.where(past, prefix_map[0, j + 1], prefix)
-        row_prefix[b] = prefix
-        distance = LANES + ids - start - lane_iota
+    def _(b):
+        code = jnp.broadcast_to(row_facts[pl.ds(b, 1), :], (rows, LANES)).T.astype(jnp.int32)
+        row_code[b] = code
+        distance = LANES + row_iota + b * rows - (code >> 11) - lane_iota
         for head in range(2):
-            terms = chain(distance, rel_bias, 2 * me + head, 0)
+            terms = bias_of(distance, head, 0)
             for r in range(2):
                 tail_bias[b, stacked(r, head), :] = terms[r * half : (r + 1) * half]
-        for part in range(3):
-            other = key_req[pl.ds(0, 1), pl.ds(pl.multiple_of(b * rows + part * LANES, LANES), LANES)]
-            same = other == number
-            cols = pl.ds(part * LANES, LANES)
-            for r in range(2):
-                same_half = same[r * half : (r + 1) * half]
-                for head in range(2):
-                    near_bias[b, stacked(r, head), cols] = jnp.where(
-                        same_half, near_bias[0, stacked(r, head), cols], masked_score
-                    )
-
-    loads[5].wait()
-
-    @pl.loop(0, w_in.shape[0] // tile)
-    def _(t):
-        cols = pl.ds(pl.multiple_of(t * tile, tile), tile)
-        w_up[:, cols] = w_in[cols, :].T
 
     first_head = lane_iota < DK
 
@@ -515,14 +496,11 @@
         for copy in incoming(make):
             copy.wait_recv()
 
-    far_bias = jnp.concatenate(
-        [jnp.full((half, 1), rel_bias[2 * me + head, 15], jnp.float32) for head in range(2)] * 2, axis=0
-    )
     far_keys = PLEN - LANES
 
     def far_scores(b):
         qh = jnp.concatenate([query_heads(b, 0), query_heads(b, 1)], axis=0)
-        choice = row_prefix[b]
+        choice = row_code[b] & 1024
         zero_first = (
             jnp.concatenate([choice[:half], choice[:half], choice[half:], choice[half:]], axis=0) == 0
         )
@@ -532,7 +510,7 @@
         )
         scores = jnp.dot(q2, k_cross[...], preferred_element_type=jnp.float32)
         scores = jnp.concatenate(
-            [scores[:, :far_keys] + far_bias, scores[:, far_keys:] + tail_bias[b]], axis=1
+            [scores[:, :far_keys], scores[:, far_keys:] + tail_bias[b]], axis=1
         )
         return zero_first, scores
 
@@ -554,6 +532,34 @@
             row_max[b] = jnp.broadcast_to(top, (2 * rows, LANES))
             row_sum[b] = jnp.broadcast_to(total, (2 * rows, LANES))
             row_acc[b] = jnp.where(zero_first, acc[:, :LANES], acc[:, LANES:])
+
+    for head in range(2):
+        for part in range(3):
+            ahead = lane_iota + (part - 1) * rows - row_iota
+            distance = jnp.abs(ahead)
+            if part == 0:
+                both = bias_of(distance, head, 0)
+            elif part == 2:
+                both = bias_of(distance, head, 16)
+            else:
+                both = jnp.where(ahead > 0, bias_of(distance, head, 16), bias_of(distance, head, 0))
+            for r in range(2):
+                near_bias[0, stacked(r, head), pl.ds(part * LANES, LANES)] = both[r * half : (r + 1) * half]
+
+    @pl.loop(0, n_req)
+    def _(step):
+        b = n_req - 1 - step
+        number = row_code[b] & 1023
+        for part in range(3):
+            other = key_req[pl.ds(0, 1), pl.ds(pl.multiple_of(b * rows + part * LANES, LANES), LANES)]
+            same = other == number
+            cols = pl.ds(part * LANES, LANES)
+            for r in range(2):
+                same_half = same[r * half : (r + 1) * half]
+                for head in range(2):
+                    near_bias[b, stacked(r, head), cols] = jnp.where(
+                        same_half, near_bias[0, stacked(r, head), cols], masked_score
+                    )
 
     for make in (k_copy, v_copy):
         for copy in incoming(make):
@@ -616,6 +622,13 @@
     home = [
         remote(far_out.at[r], far_in.at[r], f_send.at[8 + r], f_recv.at[8 + r], grp=across) for r in range(2)
     ]
+
+    loads[5].wait()
+
+    @pl.loop(0, w_in.shape[0] // tile)
+    def _(t):
+        cols = pl.ds(pl.multiple_of(t * tile, tile), tile)
+        w_up[:, cols] = w_in[cols, :].T
 
     loads[4].wait()
     for r in range(2):
@@ -752,6 +765,7 @@
             pltpu.VMEM((n_req, 2 * rows, LANES), f32),
             pltpu.VMEM((n_req, 2 * rows, 3 * LANES), f32),
             pltpu.VMEM((8, group + 2 * rows), jnp.int32),
+            pltpu.VMEM((n_req, LANES), f32),
             pltpu.VMEM((n_req, rows, LANES), jnp.int32),
             pltpu.VMEM((n_req, 2 * rows, LANES), f32),
             pltpu.VMEM((n_req, 2 * rows, LANES), f32),

time: 63.1 us -> 63.1 us (level)
  no operation moved by 1% of the time
where the time goes in v5:
time: 63.1 us; the launch traced here: 62.9 us
  Pallas kernels  61.2 us (97%)
  local copies, waits for them, and re-layouts  1.67 us (3%)
    pallas_call x1, Pallas kernels, fused(): pl.pallas_call(functools.partial(layer_kernel, n_req), out_shape=jax.Shap...  61.2 us
    unnamed x1, local copies, waits for them, and re-layouts  1.67 us

profile of v5, /device:TPU:0, one launch (start us, length us, event | category | flops | bytes accessed | tf_op | source)
XLA Modules:
  0.0 62.9 jit_solution(1547286110105775520)
XLA Ops:
  0.0 61.2 %shard_map.127 = bf16[128,1024]{1,0:T(8,128)(2,1)} custom-call(bf16[128,1024]{1,0:T(8,128)(2,1)} %tokens_hbm.1, f32[1,1024]{1,0:T(1,128)} %bitcast.4, bf16[1024,1024]{1,0:T(8,128)(2,1)} %wq_hbm.1, bf16[1024,1024]{1,0:T(8,128)(2,1)} %wk_hbm.1, bf16[1024,1024]{1,0:T(8,128)(2,1)} %wv_hbm.1, bf16[1024,1024]{1,0:T(8,128)(2,1)} %wo_hbm.1, f32[16,32]{1,0:T(8,128)} %bitcast.3, ...), custom_call_target="tpu_custom_call" | custom-call | tf_op jit(solution)/shard_map/pallas_call | solution.py:745
  61.2 1.7 %copy.15 = bf16[128,1024]{1,0:T(8,128)(2,1)} copy(bf16[128,1024]{1,0:T(8,128)(2,1)} %shard_map.127) | data formatting | bytes 524288

commit v6 on v5

--- a/solution.py
+++ b/solution.py
@@ -296,6 +296,19 @@
     piece = cache_hbm.shape[1]
     half = rows // 2
 
+    def flipped(d):
+        other, bit = 0, 1
+        while bit < n_req:
+            digit = lax.rem(lax.div(me, bit), 2)
+            other = other + bit * (1 - digit if d & bit else digit)
+            bit = 2 * bit
+        return other
+
+    far_first = list(range(n_req // 2, n_req))
+    turn_order = [far_first[0]]
+    for near_turn, far_turn in zip(range(1, n_req // 2), far_first[1:]):
+        turn_order += [near_turn, far_turn]
+
     def remote(src, dst, ssem, rsem, **where):
         return pltpu.make_async_remote_copy(
             src_ref=src, dst_ref=dst, send_sem=ssem, recv_sem=rsem, device_id=where, device_id_type=MESH
@@ -327,7 +340,7 @@
     barrier = pltpu.get_barrier_semaphore()
     for d in range(1, n_req):
         pl.semaphore_signal(
-            barrier, inc=1, device_id={"req": lax.rem(me + d, n_req)}, device_id_type=MESH
+            barrier, inc=1, device_id={"req": flipped(d)}, device_id_type=MESH
         )
     for other in (mate, across):
         pl.semaphore_signal(barrier, inc=1, device_id={"grp": other}, device_id_type=MESH)
@@ -372,12 +385,10 @@
         return make
 
     def outgoing(make):
-        return [make(d, lax.rem(me + d, n_req), me) for d in range(1, n_req)]
+        return [make(d, flipped(d), me) for d in turn_order]
 
     def incoming(make):
-        return [
-            make(d, lax.rem(me + d, n_req), lax.rem(me + n_req - d, n_req)) for d in range(1, n_req)
-        ]
+        return [make(d, flipped(d), flipped(d)) for d in turn_order]
 
     def kc_copy(d, peer, owner):
         return cache_copy(k_cache, 0, kc_send, kc_recv, d, peer, owner)
@@ -591,16 +602,16 @@
 
     near_step = 4
     for r in range(2):
-        for begin in range(1, n_req + 1, near_step):
-            turns = range(begin, begin + near_step)
-            blocks = [lax.rem(me + d, n_req) for d in turns]
+        for begin in range(0, n_req, near_step):
+            turns = (turn_order + [0])[begin : begin + near_step]
+            blocks = [flipped(d) for d in turns]
             for d, b, result in zip(turns, blocks, near(blocks, r)):
-                if d < n_req:
+                if d > 0:
                     o_send[b, parts[r], :] = result
                 else:
                     att[parts[r], lanes_of(me)] = result
             for d, b in zip(turns, blocks):
-                if d < n_req:
+                if d > 0:
                     o_copy(r)(d, b, me).start()
 
     mine = [
@@ -810,7 +821,7 @@
 
 
 def pairs_fit(mesh):
-    return mesh.shape["req"] * LANES == D and mesh.shape["grp"] == 4
+    return mesh.shape["req"] == D // LANES and mesh.shape["grp"] == 4
 
 
 def solution(mesh):

time: 63.1 us -> 63.3 us (level)
  no operation moved by 1% of the time
where the time goes in v6:
time: 63.3 us; the launch traced here: 63.1 us
  Pallas kernels  61.4 us (97%)
  local copies, waits for them, and re-layouts  1.67 us (3%)
    pallas_call x1, Pallas kernels, fused(): pl.pallas_call(functools.partial(layer_kernel, n_req), out_shape=jax.Shap...  61.4 us
    unnamed x1, local copies, waits for them, and re-layouts  1.67 us

profile of v6, /device:TPU:0, one launch (start us, length us, event | category | flops | bytes accessed | tf_op | source)
XLA Modules:
  0.0 63.1 jit_solution(18195801471043145368)
XLA Ops:
  0.0 61.4 %shard_map.127 = bf16[128,1024]{1,0:T(8,128)(2,1)} custom-call(bf16[128,1024]{1,0:T(8,128)(2,1)} %tokens_hbm.1, f32[1,1024]{1,0:T(1,128)} %bitcast.4, bf16[1024,1024]{1,0:T(8,128)(2,1)} %wq_hbm.1, bf16[1024,1024]{1,0:T(8,128)(2,1)} %wk_hbm.1, bf16[1024,1024]{1,0:T(8,128)(2,1)} %wv_hbm.1, bf16[1024,1024]{1,0:T(8,128)(2,1)} %wo_hbm.1, f32[16,32]{1,0:T(8,128)} %bitcast.3, ...), custom_call_target="tpu_custom_call" | custom-call | tf_op jit(solution)/shard_map/pallas_call | solution.py:756
  61.4 1.7 %copy.15 = bf16[128,1024]{1,0:T(8,128)(2,1)} copy(bf16[128,1024]{1,0:T(8,128)(2,1)} %shard_map.127) | data formatting | bytes 524288

commit v7 on v5

--- a/solution.py
+++ b/solution.py
@@ -403,7 +403,8 @@
     scale = lax.rsqrt(jnp.mean(wide * wide, axis=-1, keepdims=True) + epsilon)
     normed[...] = (wide * scale * attn_gain[...]).astype(jnp.bfloat16)
 
-    tile = 512
+    tile = 1024
+    turn_tile = 512
     makers = (q_copy, k_copy, v_copy)
     for part in range(3):
         loads[1 + part].wait()
@@ -625,9 +626,9 @@
 
     loads[5].wait()
 
-    @pl.loop(0, w_in.shape[0] // tile)
+    @pl.loop(0, w_in.shape[0] // turn_tile)
     def _(t):
-        cols = pl.ds(pl.multiple_of(t * tile, tile), tile)
+        cols = pl.ds(pl.multiple_of(t * turn_tile, turn_tile), turn_tile)
         w_up[:, cols] = w_in[cols, :].T
 
     loads[4].wait()

time: 63.1 us -> 61.9 us (0.981)
  Pallas kernels: 61.2 us -> 60 us
    pallas_call x1, Pallas kernels: 61.2 us -> 60 us  [fused(): pl.pallas_call(functools.partial(layer_kernel, n_req), out_shape=jax.Shap...]
where the time goes in v7:
time: 61.9 us; the launch traced here: 61.7 us
  Pallas kernels  60 us (97%)
  local copies, waits for them, and re-layouts  1.67 us (3%)
    pallas_call x1, Pallas kernels, fused(): pl.pallas_call(functools.partial(layer_kernel, n_req), out_shape=jax.Shap...  60 us
    unnamed x1, local copies, waits for them, and re-layouts  1.67 us

profile of v7, /device:TPU:0, one launch (start us, length us, event | category | flops | bytes accessed | tf_op | source)
XLA Modules:
  0.0 61.7 jit_solution(2602758249264540768)
XLA Ops:
  0.0 60.0 %shard_map.127 = bf16[128,1024]{1,0:T(8,128)(2,1)} custom-call(bf16[128,1024]{1,0:T(8,128)(2,1)} %tokens_hbm.1, f32[1,1024]{1,0:T(1,128)} %bitcast.4, bf16[1024,1024]{1,0:T(8,128)(2,1)} %wq_hbm.1, bf16[1024,1024]{1,0:T(8,128)(2,1)} %wk_hbm.1, bf16[1024,1024]{1,0:T(8,128)(2,1)} %wv_hbm.1, bf16[1024,1024]{1,0:T(8,128)(2,1)} %wo_hbm.1, f32[16,32]{1,0:T(8,128)} %bitcast.3, ...), custom_call_target="tpu_custom_call" | custom-call | tf_op jit(solution)/shard_map/pallas_call | solution.py:746
  60.0 1.7 %copy.15 = bf16[128,1024]{1,0:T(8,128)(2,1)} copy(bf16[128,1024]{1,0:T(8,128)(2,1)} %shard_map.127) | data formatting | bytes 524288
